TPU v7x, 768 devices: a whole 4x8x12 slice. The times are simulated.
768 devices in a mesh: az: 32 (over y, z_lo), rad: 12 (over x, z_hi), dep: 2 (over core).
Axes of the slice: x: 4, y: 8, z: 12 (z_hi: 3, z_lo: 4; z = z_hi * 4 + z_lo), core: 2. Of those that a mesh axis runs over, the one named last changes fastest.
Arguments:
- displacement: float32 [3, 96, 32, 4096], P(None, 'rad', 'dep', 'az'), may hold values from -3 to 3
- velocity: float32 [3, 96, 32, 4096], P(None, 'rad', 'dep', 'az'), may hold values from -4 to 4
- modulus: float32 [96, 32, 4096], P('rad', 'dep', 'az'), may hold values from 0.5 to 2
- classes: int32 [96, 32, 4096], P('rad', 'dep', 'az'), may hold values from 0 to 7
- bond_integrity: float32 [32, 96, 32, 4096], P(None, 'rad', 'dep', 'az'), may hold values from 0 to 1, as said below
- densities: float32 [8], replicated, may hold values from 0.5 to 2
- adjoint_disp: float32 [3, 96, 32, 4096], P(None, 'rad', 'dep', 'az'), may hold values from -6 to 6
- adjoint_vel: float32 [3, 96, 32, 4096], P(None, 'rad', 'dep', 'az'), may hold values from -6 to 6
Outputs:
- moved_disp: float32 [3, 96, 32, 4096], P(None, 'rad', 'dep', 'az')
- new_velocity: float32 [3, 96, 32, 4096], P(None, 'rad', 'dep', 'az')
- grad_disp: float32 [3, 96, 32, 4096], P(None, 'rad', 'dep', 'az')
- grad_vel: float32 [3, 96, 32, 4096], P(None, 'rad', 'dep', 'az')
- grad_modulus: float32 [96, 32, 4096], P('rad', 'dep', 'az')
Inputs may be any that keep to these rules, and one draw needn't show every extreme that they name: The two cells of a bond agree: bond_integrity[k, x] equals bond_integrity[31 - k, x + xi_k], with the azimuth index wrapping modulo 4096.
All inputs are finite; a program needn't handle non-finite values.
Results may differ from a plain program's by a relative error of at most 0.00002.
Values sent between devices are 32-bit elements; how exact they have to be, the bound alone decides.
A program may use at most 64 MiB of HBM per device.

v0:
```python
import math

import jax
import jax.numpy as jnp
from jax import lax
from jax.sharding import PartitionSpec as P

SOFTEN = 0.5
TIME_STEP = 0.5
BOND_OFFSETS = [
    (along_rad, along_dep, along_az)
    for along_rad in range(-2, 3)
    for along_dep in range(-2, 3)
    for along_az in range(-2, 3)
    if 0 < along_rad * along_rad + along_dep * along_dep + along_az * along_az <= 4
]


def padded(shard, sides, width, wrap):
    for axis, dim in sides:
        peers, length = (lax.axis_size(axis), shard.shape[dim])
        up = [(i, (i + 1) % peers) for i in range(peers if wrap else peers - 1)]
        down = [(j, i) for i, j in up]
        last = lax.slice_in_dim(shard, length - width, length, axis=dim)
        leading = lax.slice_in_dim(shard, 0, width, axis=dim)
        before = lax.ppermute(last, axis, up)
        after = lax.ppermute(leading, axis, down)
        shard = jnp.concatenate([before, shard, after], axis=dim)
    return shard


def extend(field):
    looped = padded(field, (("az", 3),), 2, True)
    return padded(looped, (("rad", 1), ("dep", 2)), 2, False)


def neighbour(wide, offset, shape):
    return wide[
        ...,
        2 + offset[0] : 2 + offset[0] + shape[0],
        2 + offset[1] : 2 + offset[1] + shape[1],
        2 + offset[2] : 2 + offset[2] + shape[2],
    ]


def project(offset, near, centre):
    total = jnp.zeros(centre.shape[1:], jnp.float32)
    for component in range(3):
        if offset[component] != 0:
            total = total + offset[component] * (near[component] - centre[component])
    return total


def sweep(
    centre, centre_wide, modulus, modulus_wide, bond_integrity, adjoint, adjoint_wide, with_force
):
    shape = modulus.shape
    force_parts = [jnp.zeros(shape, jnp.float32) for component in range(3)]
    turned_parts = [jnp.zeros(shape, jnp.float32) for component in range(3)]
    sensitivity = jnp.zeros(shape, jnp.float32)
    for position, offset in enumerate(BOND_OFFSETS):
        length_sq = float(offset[0] * offset[0] + offset[1] * offset[1] + offset[2] * offset[2])
        length = math.sqrt(length_sq)
        intact = bond_integrity[position]
        near_mod = neighbour(modulus_wide, offset, shape)
        stretch = project(offset, neighbour(centre_wide, offset, shape), centre) / length_sq
        bent = jnp.tanh(stretch / SOFTEN)
        total_mod = modulus + near_mod
        bond_mod = intact * (2.0 * modulus * near_mod / total_mod)
        if with_force:
            push = bond_mod * (SOFTEN / length) * bent
            for component in range(3):
                if offset[component] != 0:
                    force_parts[component] = force_parts[component] + offset[component] * push
        if adjoint is not None:
            pull = project(offset, neighbour(adjoint_wide, offset, shape), adjoint)
            stiff = bond_mod * (1.0 - bent * bent) * pull / (length_sq * length)
            for component in range(3):
                if offset[component] != 0:
                    turned_parts[component] = turned_parts[component] + offset[component] * stiff
            sensitivity = sensitivity - intact * (SOFTEN / length) * bent * pull * (
                2.0 * near_mod * near_mod / (total_mod * total_mod)
            )
    return (jnp.stack(force_parts), jnp.stack(turned_parts), sensitivity)


def shards(
    displacement, velocity, modulus, classes, bond_integrity, densities, adjoint_disp, adjoint_vel
):
    levels = jnp.arange(densities.shape[0], dtype=jnp.int32)
    density = jnp.sum(
        jnp.where(
            classes[None] == levels[:, None, None, None], densities[:, None, None, None], 0.0
        ),
        axis=0,
    )
    carried = 0.5 * TIME_STEP * adjoint_vel / density
    first = extend(jnp.concatenate([displacement, modulus[None]], axis=0))
    disp_wide = first[0:3]
    modulus_wide = first[3]
    force_start = sweep(
        displacement, disp_wide, modulus, modulus_wide, bond_integrity, None, None, True
    )[0]
    accel_start = force_start / density
    moved_disp = displacement + TIME_STEP * velocity + 0.5 * TIME_STEP * TIME_STEP * accel_start
    second = extend(jnp.concatenate([moved_disp, carried], axis=0))
    moved_wide = second[0:3]
    carried_wide = second[3:6]
    force_moved, turned_moved, sens_moved = sweep(
        moved_disp, moved_wide, modulus, modulus_wide, bond_integrity, carried, carried_wide, True
    )
    new_velocity = velocity + 0.5 * TIME_STEP * (accel_start + force_moved / density)
    total_moved = adjoint_disp + turned_moved
    grad_vel = adjoint_vel + TIME_STEP * total_moved
    back = (0.5 * TIME_STEP * adjoint_vel + 0.5 * TIME_STEP * TIME_STEP * total_moved) / density
    back_wide = extend(back)
    unused, turned_start, sens_start = sweep(
        displacement, disp_wide, modulus, modulus_wide, bond_integrity, back, back_wide, False
    )
    grad_disp = total_moved + turned_start
    grad_modulus = sens_moved + sens_start
    return (moved_disp, new_velocity, grad_disp, grad_vel, grad_modulus)


def solution(mesh):
    return jax.shard_map(
        shards,
        mesh=mesh,
        in_specs=(
            P(None, "rad", "dep", "az"),
            P(None, "rad", "dep", "az"),
            P("rad", "dep", "az"),
            P("rad", "dep", "az"),
            P(None, "rad", "dep", "az"),
            P(),
            P(None, "rad", "dep", "az"),
            P(None, "rad", "dep", "az"),
        ),
        out_specs=(
            P(None, "rad", "dep", "az"),
            P(None, "rad", "dep", "az"),
            P(None, "rad", "dep", "az"),
            P(None, "rad", "dep", "az"),
            P("rad", "dep", "az"),
        ),
        check_vma=False,
    )
```

profile of v0, /device:TPU:41, one launch (start us, length us, event | category | flops | bytes accessed | tf_op | source)
XLA Modules:
  0.0 180.9 jit_solution(13648530462277994046)
XLA Ops:
  0.7 1.3 slice_maximum_fusion.1
  2.0 4.0 %collective-permute-start = (f32[4,8,16,2]{3,2,1,0:T(8,128)S(1)}, f32[4,8,16,2]{3,2,1,0:T(8,128)S(1)}, u32[]{:S(2)}, u32[]{:S(2)}) collective-permute-start(f32[4,8,16,2]{3,2,1,0:T(8,128)S(1)} %get-tuple-element.193), channel_id=1, source_target_pairs={{0,24},{24,48},{48,72},{72,96},{96,120},{120,144},{144,168},{168,1... | collective-permute-start | bytes 12296 | tf_op jit(solution)/shard_map/ppermute | solution.py:26
  6.0 6.3 %collective-permute-start.1 = (f32[4,8,16,2]{3,2,1,0:T(8,128)S(1)}, f32[4,8,16,2]{3,2,1,0:T(8,128)S(1)}, u32[]{:S(2)}, u32[]{:S(2)}) collective-permute-start(f32[4,8,16,2]{3,2,1,0:T(8,128)S(1)} %get-tuple-element.194), channel_id=1, source_target_pairs={{24,0},{48,24},{72,48},{96,72},{120,96},{144,120},{168,144},{192,1... | collective-permute-start | bytes 12296 | tf_op jit(solution)/shard_map/ppermute | solution.py:27
  12.3 4.2 %collective-permute-done = f32[4,8,16,2]{3,2,1,0:T(8,128)S(1)} collective-permute-done((f32[4,8,16,2]{3,2,1,0:T(8,128)S(1)}, f32[4,8,16,2]{3,2,1,0:T(8,128)S(1)}, u32[]{:S(2)}, u32[]{:S(2)}) %collective-permute-start) | collective-permute-done | bytes 4128 | tf_op jit(solution)/shard_map/ppermute | solution.py:26
  16.5 5.5 %collective-permute-done.1 = f32[4,8,16,2]{3,2,1,0:T(8,128)S(1)} collective-permute-done((f32[4,8,16,2]{3,2,1,0:T(8,128)S(1)}, f32[4,8,16,2]{3,2,1,0:T(8,128)S(1)}, u32[]{:S(2)}, u32[]{:S(2)}) %collective-permute-start.1) | collective-permute-done | bytes 4128 | tf_op jit(solution)/shard_map/ppermute | solution.py:27
  21.9 1.0 pad_maximum_fusion.18
  23.0 10.3 %collective-permute-start.2 = (f32[4,2,16,132]{3,2,1,0:T(8,128)S(1)}, f32[4,2,16,132]{3,2,1,0:T(8,128)S(1)}, u32[]{:S(2)}, u32[]{:S(2)}) collective-permute-start(f32[4,2,16,132]{3,2,1,0:T(8,128)S(1)} %get-tuple-element.185), channel_id=1, source_target_pairs={{0,2},{2,4},{4,6},{6,8},{8,10},{10,12},{12,14},{14,16},{16,18},{18... | collective-permute-start | bytes 202760 | tf_op jit(solution)/shard_map/ppermute | solution.py:26
  33.3 1.3 collective-permute-start.3
  34.6 6.6 %collective-permute-done.2 = f32[4,2,16,132]{3,2,1,0:T(8,128)S(1)} collective-permute-done((f32[4,2,16,132]{3,2,1,0:T(8,128)S(1)}, f32[4,2,16,132]{3,2,1,0:T(8,128)S(1)}, u32[]{:S(2)}, u32[]{:S(2)}) %collective-permute-start.2) | collective-permute-done | bytes 67616 | tf_op jit(solution)/shard_map/ppermute | solution.py:26
  41.3 10.9 %collective-permute-done.3 = f32[4,2,16,132]{3,2,1,0:T(8,128)S(1)} collective-permute-done((f32[4,2,16,132]{3,2,1,0:T(8,128)S(1)}, f32[4,2,16,132]{3,2,1,0:T(8,128)S(1)}, u32[]{:S(2)}, u32[]{:S(2)}) %collective-permute-start.3) | collective-permute-done | bytes 67616 | tf_op jit(solution)/shard_map/ppermute | solution.py:27
  52.2 0.3 pad_maximum_fusion.27
  52.5 1.3 collective-permute-start.4
  53.8 3.0 %collective-permute-start.5 = (f32[4,12,2,132]{3,2,1,0:T(2,128)S(1)}, f32[4,12,2,132]{3,2,1,0:T(2,128)S(1)}, u32[]{:S(2)}, u32[]{:S(2)}) collective-permute-start(f32[4,12,2,132]{3,2,1,0:T(2,128)S(1)} %get-tuple-element.180), channel_id=1, source_target_pairs={{1,0},{3,2},{5,4},{7,6},{9,8},{11,10},{13,12},{15,14},{17,16},{19,... | collective-permute-start | bytes 152072 | tf_op jit(solution)/shard_map/ppermute | solution.py:27
  57.0 0.8 collective-permute-done.5
  57.7 0.1 fusion.7
  57.9 0.6 pad_maximum_fusion.1
  58.5 1.0 copy-done.2
  59.5 1.3 add_bitcast_fusion.11
  60.8 0.5 add_bitcast_fusion.10
  61.4 1.1 add_bitcast_fusion.9
  62.6 0.2 slice_maximum_fusion
  62.8 1.9 %collective-permute-start.6 = (f32[6,8,16,2]{3,2,1,0:T(8,128)S(1)}, f32[6,8,16,2]{3,2,1,0:T(8,128)S(1)}, u32[]{:S(2)}, u32[]{:S(2)}) collective-permute-start(f32[6,8,16,2]{3,2,1,0:T(8,128)S(1)} %get-tuple-element.191), channel_id=1, source_target_pairs={{0,24},{24,48},{48,72},{72,96},{96,120},{120,144},{144,168},{168,1... | collective-permute-start | bytes 18440 | tf_op jit(solution)/shard_map/ppermute | solution.py:26
  64.7 6.1 %collective-permute-start.7 = (f32[6,8,16,2]{3,2,1,0:T(8,128)S(1)}, f32[6,8,16,2]{3,2,1,0:T(8,128)S(1)}, u32[]{:S(2)}, u32[]{:S(2)}) collective-permute-start(f32[6,8,16,2]{3,2,1,0:T(8,128)S(1)} %get-tuple-element.192), channel_id=1, source_target_pairs={{24,0},{48,24},{72,48},{96,72},{120,96},{144,120},{168,144},{192,1... | collective-permute-start | bytes 18440 | tf_op jit(solution)/shard_map/ppermute | solution.py:27
  70.8 7.0 %collective-permute-done.6 = f32[6,8,16,2]{3,2,1,0:T(8,128)S(1)} collective-permute-done((f32[6,8,16,2]{3,2,1,0:T(8,128)S(1)}, f32[6,8,16,2]{3,2,1,0:T(8,128)S(1)}, u32[]{:S(2)}, u32[]{:S(2)}) %collective-permute-start.6) | collective-permute-done | bytes 6176 | tf_op jit(solution)/shard_map/ppermute | solution.py:26
  77.8 8.2 %collective-permute-done.7 = f32[6,8,16,2]{3,2,1,0:T(8,128)S(1)} collective-permute-done((f32[6,8,16,2]{3,2,1,0:T(8,128)S(1)}, f32[6,8,16,2]{3,2,1,0:T(8,128)S(1)}, u32[]{:S(2)}, u32[]{:S(2)}) %collective-permute-start.7) | collective-permute-done | bytes 6176 | tf_op jit(solution)/shard_map/ppermute | solution.py:27
  86.0 0.2 pad_maximum_fusion.5
  86.2 1.3 collective-permute-start.9
  87.5 7.9 %collective-permute-start.8 = (f32[6,2,16,132]{3,2,1,0:T(8,128)S(1)}, f32[6,2,16,132]{3,2,1,0:T(8,128)S(1)}, u32[]{:S(2)}, u32[]{:S(2)}) collective-permute-start(f32[6,2,16,132]{3,2,1,0:T(8,128)S(1)} %get-tuple-element.176), channel_id=1, source_target_pairs={{0,2},{2,4},{4,6},{6,8},{8,10},{10,12},{12,14},{14,16},{16,18},{18... | collective-permute-start | bytes 304136 | tf_op jit(solution)/shard_map/ppermute | solution.py:26
  95.4 15.0 %collective-permute-done.9 = f32[6,2,16,132]{3,2,1,0:T(8,128)S(1)} collective-permute-done((f32[6,2,16,132]{3,2,1,0:T(8,128)S(1)}, f32[6,2,16,132]{3,2,1,0:T(8,128)S(1)}, u32[]{:S(2)}, u32[]{:S(2)}) %collective-permute-start.9) | collective-permute-done | bytes 101408 | tf_op jit(solution)/shard_map/ppermute | solution.py:27
  110.4 2.0 %collective-permute-done.8 = f32[6,2,16,132]{3,2,1,0:T(8,128)S(1)} collective-permute-done((f32[6,2,16,132]{3,2,1,0:T(8,128)S(1)}, f32[6,2,16,132]{3,2,1,0:T(8,128)S(1)}, u32[]{:S(2)}, u32[]{:S(2)}) %collective-permute-start.8) | collective-permute-done | bytes 101408 | tf_op jit(solution)/shard_map/ppermute | solution.py:26
  112.4 0.4 pad_maximum_fusion.9
  112.8 2.4 %collective-permute-start.11 = (f32[6,12,2,132]{3,2,1,0:T(2,128)S(1)}, f32[6,12,2,132]{3,2,1,0:T(2,128)S(1)}, u32[]{:S(2)}, u32[]{:S(2)}) collective-permute-start(f32[6,12,2,132]{3,2,1,0:T(2,128)S(1)} %get-tuple-element.173), channel_id=1, source_target_pairs={{1,0},{3,2},{5,4},{7,6},{9,8},{11,10},{13,12},{15,14},{17,16},{19,... | collective-permute-start | bytes 228104 | tf_op jit(solution)/shard_map/ppermute | solution.py:27
  115.2 1.3 collective-permute-start.10
  116.5 2.0 %collective-permute-done.10 = f32[6,12,2,132]{3,2,1,0:T(2,128)S(1)} collective-permute-done((f32[6,12,2,132]{3,2,1,0:T(2,128)S(1)}, f32[6,12,2,132]{3,2,1,0:T(2,128)S(1)}, u32[]{:S(2)}, u32[]{:S(2)}) %collective-permute-start.10) | collective-permute-done | bytes 76064 | tf_op jit(solution)/shard_map/ppermute | solution.py:26
  118.5 1.9 %pad_maximum_fusion = (f32[6,12,18,132]{3,2,1,0:T(8,128)S(1)}, f32[6,12,18,132]{3,2,1,0:T(8,128)S(1)}) fusion(f32[6,12,2,132]{3,2,1,0:T(2,128)S(1)} %collective-permute-done.11, f32[6,2,16,132]{3,2,1,0:T(8,128)S(1)} %collective-permute-done.9, f32[6,8,16,2]{3,2,1,0:T(8,128)S(1)} %collective-permute-done.7, f32[3,8,16,128]{3,2,1,0:T(8,128)S(1)} %get-tuple-element.200, ...), kind=kLoop, calls=%fused_computation.1 | loop fusion | flops 2052864 | bytes 2128896 | tf_op jit(solution)/shard_map/concatenate | solution.py:28
  120.3 0.2 fusion.267
  120.6 0.2 fusion.302
  120.8 0.2 fusion.346
  121.0 2.7 %add_bitcast_fusion.5 = (f32[1,8,16,128]{3,2,1,0:T(8,128)}, f32[8,16,128]{2,1,0:T(8,128)}, f32[8,16,128]{2,1,0:T(8,128)}, f32[8,16,128]{2,1,0:T(8,128)}, f32[8,1...) fusion(f32[8,16,128]{2,1,0:T(8,128)S(1)} %get-tuple-element.106, ...), kind=kLoop, calls=%fused_computation.917 | loop fusion | flops 5521408 | bytes 9109504 | tf_op jit(solution)/shard_map/stack | solution.py:84
  123.6 1.4 add_bitcast_fusion.4
  125.1 0.3 add_bitcast_fusion.7
  125.4 0.5 copy-done.17
  126.0 0.2 add_bitcast_fusion.8
  126.2 0.4 add_bitcast_fusion.3
  126.7 0.2 add_bitcast_fusion.6
  126.9 0.6 copy-done.6
  127.7 0.8 multiply_add_fusion
  128.6 1.9 %collective-permute-start.12 = (f32[3,8,16,2]{3,2,1,0:T(8,128)S(1)}, f32[3,8,16,2]{3,2,1,0:T(8,128)S(1)}, u32[]{:S(2)}, u32[]{:S(2)}) collective-permute-start(f32[3,8,16,2]{3,2,1,0:T(8,128)S(1)} %get-tuple-element.195), channel_id=1, source_target_pairs={{0,24},{24,48},{48,72},{72,96},{96,120},{120,144},{144,168},{168,1... | collective-permute-start | bytes 9224 | tf_op jit(solution)/shard_map/ppermute | solution.py:26
  130.5 6.1 %collective-permute-start.13 = (f32[3,8,16,2]{3,2,1,0:T(8,128)S(1)}, f32[3,8,16,2]{3,2,1,0:T(8,128)S(1)}, u32[]{:S(2)}, u32[]{:S(2)}) collective-permute-start(f32[3,8,16,2]{3,2,1,0:T(8,128)S(1)} %get-tuple-element.196), channel_id=1, source_target_pairs={{24,0},{48,24},{72,48},{96,72},{120,96},{144,120},{168,144},{192,1... | collective-permute-start | bytes 9224 | tf_op jit(solution)/shard_map/ppermute | solution.py:27
  136.6 2.9 %collective-permute-done.12 = f32[3,8,16,2]{3,2,1,0:T(8,128)S(1)} collective-permute-done((f32[3,8,16,2]{3,2,1,0:T(8,128)S(1)}, f32[3,8,16,2]{3,2,1,0:T(8,128)S(1)}, u32[]{:S(2)}, u32[]{:S(2)}) %collective-permute-start.12) | collective-permute-done | bytes 3104 | tf_op jit(solution)/shard_map/ppermute | solution.py:26
  139.5 3.9 %collective-permute-done.13 = f32[3,8,16,2]{3,2,1,0:T(8,128)S(1)} collective-permute-done((f32[3,8,16,2]{3,2,1,0:T(8,128)S(1)}, f32[3,8,16,2]{3,2,1,0:T(8,128)S(1)}, u32[]{:S(2)}, u32[]{:S(2)}) %collective-permute-start.13) | collective-permute-done | bytes 3104 | tf_op jit(solution)/shard_map/ppermute | solution.py:27
  143.6 8.0 %collective-permute-start.14 = (f32[3,2,16,132]{3,2,1,0:T(8,128)S(1)}, f32[3,2,16,132]{3,2,1,0:T(8,128)S(1)}, u32[]{:S(2)}, u32[]{:S(2)}) collective-permute-start(f32[3,2,16,132]{3,2,1,0:T(8,128)S(1)} %get-tuple-element.189), channel_id=1, source_target_pairs={{0,2},{2,4},{4,6},{6,8},{8,10},{10,12},{12,14},{14,16},{16,18},{18... | collective-permute-start | bytes 152072 | tf_op jit(solution)/shard_map/ppermute | solution.py:26
  151.8 1.4 collective-permute-start.15
  153.3 14.5 %collective-permute-done.15 = f32[3,2,16,132]{3,2,1,0:T(8,128)S(1)} collective-permute-done((f32[3,2,16,132]{3,2,1,0:T(8,128)S(1)}, f32[3,2,16,132]{3,2,1,0:T(8,128)S(1)}, u32[]{:S(2)}, u32[]{:S(2)}) %collective-permute-start.15) | collective-permute-done | bytes 50720 | tf_op jit(solution)/shard_map/ppermute | solution.py:27
  167.8 0.2 pad_maximum_fusion.32
  168.0 1.3 collective-permute-start.16
  169.3 3.0 %collective-permute-start.17 = (f32[3,12,2,132]{3,2,1,0:T(2,128)S(1)}, f32[3,12,2,132]{3,2,1,0:T(2,128)S(1)}, u32[]{:S(2)}, u32[]{:S(2)}) collective-permute-start(f32[3,12,2,132]{3,2,1,0:T(2,128)S(1)} %get-tuple-element.184), channel_id=1, source_target_pairs={{1,0},{3,2},{5,4},{7,6},{9,8},{11,10},{13,12},{15,14},{17,16},{19,... | collective-permute-start | bytes 114056 | tf_op jit(solution)/shard_map/ppermute | solution.py:27
  172.3 0.9 collective-permute-done.17
  173.2 0.5 maximum_maximum_fusion.2
  173.8 5.3 %subtract_add_fusion = (f32[8,16,128]{2,1,0:T(8,128)}, f32[8,16,128]{2,1,0:T(8,128)S(1)}, f32[8,16,128]{2,1,0:T(8,128)S(1)}, f32[8,16,128]{2,1,0:T(8,128)S(1)}, ...) fusion(f32[8,16,128]{2,1,0:T(8,128)S(1)} %get-tuple-element.110, ...), kind=kLoop, calls=%fused_computation.887 | loop fusion | flops 10240000 | bytes 16515072 | tf_op jit(solution)/shard_map/add | solution.py:121
  179.2 0.4 add_bitcast_fusion.2
  179.6 0.3 add_bitcast_fusion.1
  179.9 0.3 add_bitcast_fusion
  180.2 0.7 maximum_add_fusion.1
  (83 shorter events, 0.9 us)
Async XLA Ops:
  0.6 51.6 %copy-start.1 = (f32[3,8,16,128]{3,2,1,0:T(8,128)S(1)}, f32[3,8,16,128]{3,2,1,0:T(8,128)}, u32[]{:S(2)}) copy-start(f32[3,8,16,128]{3,2,1,0:T(8,128)} %param.8) | copy-start | bytes 589828
  0.6 51.6 %copy-start.3 = (f32[8,16,128]{2,1,0:T(8,128)S(1)}, f32[8,16,128]{2,1,0:T(8,128)}, u32[]{:S(2)}) copy-start(f32[8,16,128]{2,1,0:T(8,128)} %param.10) | copy-start | bytes 196612
  0.7 56.2 %copy-start.38 = (f32[8]{0:T(128)S(1)}, f32[8]{0:T(128)}, u32[]{:S(2)}) copy-start(f32[8]{0:T(128)} %param.13) | copy-start | bytes 100
  0.7 56.2 %copy-start.37 = (s32[8,16,128]{2,1,0:T(8,128)S(1)}, s32[8,16,128]{2,1,0:T(8,128)}, u32[]{:S(2)}) copy-start(s32[8,16,128]{2,1,0:T(8,128)} %param.11) | copy-start | bytes 196612
  2.0 14.5 %collective-permute-start = (f32[4,8,16,2]{3,2,1,0:T(8,128)S(1)}, f32[4,8,16,2]{3,2,1,0:T(8,128)S(1)}, u32[]{:S(2)}, u32[]{:S(2)}) collective-permute-start(f32[4,8,16,2]{3,2,1,0:T(8,128)S(1)} %get-tuple-element.193), channel_id=1, source_target_pairs={{0,24},{24,48},{48,72},{72,96},{96,120},{120,144},{144,168},{168,1... | collective-permute-start | bytes 12296 | tf_op jit(solution)/shard_map/ppermute | solution.py:26
  6.0 16.0 %collective-permute-start.1 = (f32[4,8,16,2]{3,2,1,0:T(8,128)S(1)}, f32[4,8,16,2]{3,2,1,0:T(8,128)S(1)}, u32[]{:S(2)}, u32[]{:S(2)}) collective-permute-start(f32[4,8,16,2]{3,2,1,0:T(8,128)S(1)} %get-tuple-element.194), channel_id=1, source_target_pairs={{24,0},{48,24},{72,48},{96,72},{120,96},{144,120},{168,144},{192,1... | collective-permute-start | bytes 12296 | tf_op jit(solution)/shard_map/ppermute | solution.py:27
  23.0 18.3 %collective-permute-start.2 = (f32[4,2,16,132]{3,2,1,0:T(8,128)S(1)}, f32[4,2,16,132]{3,2,1,0:T(8,128)S(1)}, u32[]{:S(2)}, u32[]{:S(2)}) collective-permute-start(f32[4,2,16,132]{3,2,1,0:T(8,128)S(1)} %get-tuple-element.185), channel_id=1, source_target_pairs={{0,2},{2,4},{4,6},{6,8},{8,10},{10,12},{12,14},{14,16},{16,18},{18... | collective-permute-start | bytes 202760 | tf_op jit(solution)/shard_map/ppermute | solution.py:26
  33.3 18.9 %collective-permute-start.3 = (f32[4,2,16,132]{3,2,1,0:T(8,128)S(1)}, f32[4,2,16,132]{3,2,1,0:T(8,128)S(1)}, u32[]{:S(2)}, u32[]{:S(2)}) collective-permute-start(f32[4,2,16,132]{3,2,1,0:T(8,128)S(1)} %get-tuple-element.186), channel_id=1, source_target_pairs={{2,0},{4,2},{6,4},{8,6},{10,8},{12,10},{14,12},{16,14},{18,16},{20... | collective-permute-start | bytes 202760 | tf_op jit(solution)/shard_map/ppermute | solution.py:27
  52.5 4.5 %collective-permute-start.4 = (f32[4,12,2,132]{3,2,1,0:T(2,128)S(1)}, f32[4,12,2,132]{3,2,1,0:T(2,128)S(1)}, u32[]{:S(2)}, u32[]{:S(2)}) collective-permute-start(f32[4,12,2,132]{3,2,1,0:T(2,128)S(1)} %get-tuple-element.179), channel_id=1, source_target_pairs={{0,1},{2,3},{4,5},{6,7},{8,9},{10,11},{12,13},{14,15},{16,17},{18,... | collective-permute-start | bytes 152072 | tf_op jit(solution)/shard_map/ppermute | solution.py:26
  53.8 4.0 %collective-permute-start.5 = (f32[4,12,2,132]{3,2,1,0:T(2,128)S(1)}, f32[4,12,2,132]{3,2,1,0:T(2,128)S(1)}, u32[]{:S(2)}, u32[]{:S(2)}) collective-permute-start(f32[4,12,2,132]{3,2,1,0:T(2,128)S(1)} %get-tuple-element.180), channel_id=1, source_target_pairs={{1,0},{3,2},{5,4},{7,6},{9,8},{11,10},{13,12},{15,14},{17,16},{19,... | collective-permute-start | bytes 152072 | tf_op jit(solution)/shard_map/ppermute | solution.py:27
  57.0 5.5 %copy-start.23 = (f32[8,16,128]{2,1,0:T(8,128)}, f32[8,16,128]{2,1,0:T(8,128)S(1)}, u32[]{:S(2)}) copy-start(f32[8,16,128]{2,1,0:T(8,128)S(1)} %select_reduce_fusion) | copy-start | bytes 196612
  57.9 1.6 copy-start.2
  60.8 1.6 copy-start.13
  61.4 1.1 copy-start.15
  61.4 1.1 copy-start.4
  61.4 1.1 copy-start.5
  62.5 23.7 %copy-start.21 = (f32[1,8,16,128]{3,2,1,0:T(8,128)}, f32[1,8,16,128]{3,2,1,0:T(8,128)S(1)}, u32[]{:S(2)}) copy-start(f32[1,8,16,128]{3,2,1,0:T(8,128)S(1)} %get-tuple-element.156) | copy-start | bytes 196612
  62.6 111.1 %copy-start = (f32[3,8,16,128]{3,2,1,0:T(8,128)}, f32[3,8,16,128]{3,2,1,0:T(8,128)S(1)}, u32[]{:S(2)}) copy-start(f32[3,8,16,128]{3,2,1,0:T(8,128)S(1)} %get-tuple-element.201) | copy-start | bytes 589828
  62.8 15.0 %collective-permute-start.6 = (f32[6,8,16,2]{3,2,1,0:T(8,128)S(1)}, f32[6,8,16,2]{3,2,1,0:T(8,128)S(1)}, u32[]{:S(2)}, u32[]{:S(2)}) collective-permute-start(f32[6,8,16,2]{3,2,1,0:T(8,128)S(1)} %get-tuple-element.191), channel_id=1, source_target_pairs={{0,24},{24,48},{48,72},{72,96},{96,120},{120,144},{144,168},{168,1... | collective-permute-start | bytes 18440 | tf_op jit(solution)/shard_map/ppermute | solution.py:26
  64.7 21.2 %collective-permute-start.7 = (f32[6,8,16,2]{3,2,1,0:T(8,128)S(1)}, f32[6,8,16,2]{3,2,1,0:T(8,128)S(1)}, u32[]{:S(2)}, u32[]{:S(2)}) collective-permute-start(f32[6,8,16,2]{3,2,1,0:T(8,128)S(1)} %get-tuple-element.192), channel_id=1, source_target_pairs={{24,0},{48,24},{72,48},{96,72},{120,96},{144,120},{168,144},{192,1... | collective-permute-start | bytes 18440 | tf_op jit(solution)/shard_map/ppermute | solution.py:27
  86.2 24.2 %collective-permute-start.9 = (f32[6,2,16,132]{3,2,1,0:T(8,128)S(1)}, f32[6,2,16,132]{3,2,1,0:T(8,128)S(1)}, u32[]{:S(2)}, u32[]{:S(2)}) collective-permute-start(f32[6,2,16,132]{3,2,1,0:T(8,128)S(1)} %get-tuple-element.175), channel_id=1, source_target_pairs={{2,0},{4,2},{6,4},{8,6},{10,8},{12,10},{14,12},{16,14},{18,16},{20... | collective-permute-start | bytes 304136 | tf_op jit(solution)/shard_map/ppermute | solution.py:27
  87.5 24.9 %collective-permute-start.8 = (f32[6,2,16,132]{3,2,1,0:T(8,128)S(1)}, f32[6,2,16,132]{3,2,1,0:T(8,128)S(1)}, u32[]{:S(2)}, u32[]{:S(2)}) collective-permute-start(f32[6,2,16,132]{3,2,1,0:T(8,128)S(1)} %get-tuple-element.176), channel_id=1, source_target_pairs={{0,2},{2,4},{4,6},{6,8},{8,10},{10,12},{12,14},{14,16},{16,18},{18... | collective-permute-start | bytes 304136 | tf_op jit(solution)/shard_map/ppermute | solution.py:26
  112.8 3.7 %collective-permute-start.11 = (f32[6,12,2,132]{3,2,1,0:T(2,128)S(1)}, f32[6,12,2,132]{3,2,1,0:T(2,128)S(1)}, u32[]{:S(2)}, u32[]{:S(2)}) collective-permute-start(f32[6,12,2,132]{3,2,1,0:T(2,128)S(1)} %get-tuple-element.173), channel_id=1, source_target_pairs={{1,0},{3,2},{5,4},{7,6},{9,8},{11,10},{13,12},{15,14},{17,16},{19,... | collective-permute-start | bytes 228104 | tf_op jit(solution)/shard_map/ppermute | solution.py:27
  115.2 3.3 %collective-permute-start.10 = (f32[6,12,2,132]{3,2,1,0:T(2,128)S(1)}, f32[6,12,2,132]{3,2,1,0:T(2,128)S(1)}, u32[]{:S(2)}, u32[]{:S(2)}) collective-permute-start(f32[6,12,2,132]{3,2,1,0:T(2,128)S(1)} %get-tuple-element.174), channel_id=1, source_target_pairs={{0,1},{2,3},{4,5},{6,7},{8,9},{10,11},{12,13},{14,15},{16,17},{18,... | collective-permute-start | bytes 228104 | tf_op jit(solution)/shard_map/ppermute | solution.py:26
  125.0 0.8 copy-start.17
  125.0 0.9 copy-start.18
  125.1 0.9 copy-start.19
  125.1 0.9 copy-start.20
  125.3 0.9 copy-start.7
  126.6 0.9 copy-start.6
  126.6 0.9 copy-start.12
  126.6 0.9 copy-start.14
  126.6 1.0 copy-start.16
  126.6 1.0 copy-start.22
  126.6 1.0 copy-start.24
  128.6 10.9 %collective-permute-start.12 = (f32[3,8,16,2]{3,2,1,0:T(8,128)S(1)}, f32[3,8,16,2]{3,2,1,0:T(8,128)S(1)}, u32[]{:S(2)}, u32[]{:S(2)}) collective-permute-start(f32[3,8,16,2]{3,2,1,0:T(8,128)S(1)} %get-tuple-element.195), channel_id=1, source_target_pairs={{0,24},{24,48},{48,72},{72,96},{96,120},{120,144},{144,168},{168,1... | collective-permute-start | bytes 9224 | tf_op jit(solution)/shard_map/ppermute | solution.py:26
  130.5 12.9 %collective-permute-start.13 = (f32[3,8,16,2]{3,2,1,0:T(8,128)S(1)}, f32[3,8,16,2]{3,2,1,0:T(8,128)S(1)}, u32[]{:S(2)}, u32[]{:S(2)}) collective-permute-start(f32[3,8,16,2]{3,2,1,0:T(8,128)S(1)} %get-tuple-element.196), channel_id=1, source_target_pairs={{24,0},{48,24},{72,48},{96,72},{120,96},{144,120},{168,144},{192,1... | collective-permute-start | bytes 9224 | tf_op jit(solution)/shard_map/ppermute | solution.py:27
  143.6 9.7 %collective-permute-start.14 = (f32[3,2,16,132]{3,2,1,0:T(8,128)S(1)}, f32[3,2,16,132]{3,2,1,0:T(8,128)S(1)}, u32[]{:S(2)}, u32[]{:S(2)}) collective-permute-start(f32[3,2,16,132]{3,2,1,0:T(8,128)S(1)} %get-tuple-element.189), channel_id=1, source_target_pairs={{0,2},{2,4},{4,6},{6,8},{8,10},{10,12},{12,14},{14,16},{16,18},{18... | collective-permute-start | bytes 152072 | tf_op jit(solution)/shard_map/ppermute | solution.py:26
  151.6 22.0 %copy-start.8 = (f32[8,16,128]{2,1,0:T(8,128)S(1)}, f32[8,16,128]{2,1,0:T(8,128)}, u32[]{:S(2)}) copy-start(f32[8,16,128]{2,1,0:T(8,128)} %get-tuple-element.161) | copy-start | bytes 196612
  151.6 22.0 %copy-start.9 = (f32[8,16,128]{2,1,0:T(8,128)S(1)}, f32[8,16,128]{2,1,0:T(8,128)}, u32[]{:S(2)}) copy-start(f32[8,16,128]{2,1,0:T(8,128)} %get-tuple-element.162) | copy-start | bytes 196612
  151.7 22.0 %copy-start.10 = (f32[8,16,128]{2,1,0:T(8,128)S(1)}, f32[8,16,128]{2,1,0:T(8,128)}, u32[]{:S(2)}) copy-start(f32[8,16,128]{2,1,0:T(8,128)} %get-tuple-element.163) | copy-start | bytes 196612
  151.7 22.0 %copy-start.11 = (f32[8,16,128]{2,1,0:T(8,128)S(1)}, f32[8,16,128]{2,1,0:T(8,128)}, u32[]{:S(2)}) copy-start(f32[8,16,128]{2,1,0:T(8,128)} %get-tuple-element.164) | copy-start | bytes 196612
  151.7 22.0 %copy-start.25 = (f32[8,16,128]{2,1,0:T(8,128)S(1)}, f32[8,16,128]{2,1,0:T(8,128)}, u32[]{:S(2)}) copy-start(f32[8,16,128]{2,1,0:T(8,128)} %get-tuple-element.44) | copy-start | bytes 196612
  151.7 22.0 %copy-start.26 = (f32[8,16,128]{2,1,0:T(8,128)S(1)}, f32[8,16,128]{2,1,0:T(8,128)}, u32[]{:S(2)}) copy-start(f32[8,16,128]{2,1,0:T(8,128)} %get-tuple-element.45) | copy-start | bytes 196612
  151.7 22.0 %copy-start.27 = (f32[8,16,128]{2,1,0:T(8,128)S(1)}, f32[8,16,128]{2,1,0:T(8,128)}, u32[]{:S(2)}) copy-start(f32[8,16,128]{2,1,0:T(8,128)} %get-tuple-element.46) | copy-start | bytes 196612
  151.7 22.0 %copy-start.28 = (f32[8,16,128]{2,1,0:T(8,128)S(1)}, f32[8,16,128]{2,1,0:T(8,128)}, u32[]{:S(2)}) copy-start(f32[8,16,128]{2,1,0:T(8,128)} %get-tuple-element.47) | copy-start | bytes 196612
  151.7 22.0 %copy-start.29 = (f32[8,16,128]{2,1,0:T(8,128)S(1)}, f32[8,16,128]{2,1,0:T(8,128)}, u32[]{:S(2)}) copy-start(f32[8,16,128]{2,1,0:T(8,128)} %get-tuple-element.57) | copy-start | bytes 196612
  151.7 22.0 %copy-start.30 = (f32[8,16,128]{2,1,0:T(8,128)S(1)}, f32[8,16,128]{2,1,0:T(8,128)}, u32[]{:S(2)}) copy-start(f32[8,16,128]{2,1,0:T(8,128)} %get-tuple-element.59) | copy-start | bytes 196612
  151.7 22.0 %copy-start.31 = (f32[8,16,128]{2,1,0:T(8,128)S(1)}, f32[8,16,128]{2,1,0:T(8,128)}, u32[]{:S(2)}) copy-start(f32[8,16,128]{2,1,0:T(8,128)} %get-tuple-element.61) | copy-start | bytes 196612
  151.8 22.0 %copy-start.32 = (f32[8,16,128]{2,1,0:T(8,128)S(1)}, f32[8,16,128]{2,1,0:T(8,128)}, u32[]{:S(2)}) copy-start(f32[8,16,128]{2,1,0:T(8,128)} %get-tuple-element.63) | copy-start | bytes 196612
  151.8 22.0 %copy-start.33 = (f32[8,16,128]{2,1,0:T(8,128)S(1)}, f32[8,16,128]{2,1,0:T(8,128)}, u32[]{:S(2)}) copy-start(f32[8,16,128]{2,1,0:T(8,128)} %get-tuple-element.65) | copy-start | bytes 196612
  151.8 22.0 %copy-start.34 = (f32[8,16,128]{2,1,0:T(8,128)S(1)}, f32[8,16,128]{2,1,0:T(8,128)}, u32[]{:S(2)}) copy-start(f32[8,16,128]{2,1,0:T(8,128)} %get-tuple-element.67) | copy-start | bytes 196612
  151.8 22.0 %copy-start.35 = (f32[8,16,128]{2,1,0:T(8,128)S(1)}, f32[8,16,128]{2,1,0:T(8,128)}, u32[]{:S(2)}) copy-start(f32[8,16,128]{2,1,0:T(8,128)} %get-tuple-element.69) | copy-start | bytes 196612
  151.8 22.0 %copy-start.36 = (f32[8,16,128]{2,1,0:T(8,128)S(1)}, f32[8,16,128]{2,1,0:T(8,128)}, u32[]{:S(2)}) copy-start(f32[8,16,128]{2,1,0:T(8,128)} %get-tuple-element.71) | copy-start | bytes 196612
  151.8 16.0 %collective-permute-start.15 = (f32[3,2,16,132]{3,2,1,0:T(8,128)S(1)}, f32[3,2,16,132]{3,2,1,0:T(8,128)S(1)}, u32[]{:S(2)}, u32[]{:S(2)}) collective-permute-start(f32[3,2,16,132]{3,2,1,0:T(8,128)S(1)} %get-tuple-element.190), channel_id=1, source_target_pairs={{2,0},{4,2},{6,4},{8,6},{10,8},{12,10},{14,12},{16,14},{18,16},{20... | collective-permute-start | bytes 152072 | tf_op jit(solution)/shard_map/ppermute | solution.py:27
  168.0 4.3 %collective-permute-start.16 = (f32[3,12,2,132]{3,2,1,0:T(2,128)S(1)}, f32[3,12,2,132]{3,2,1,0:T(2,128)S(1)}, u32[]{:S(2)}, u32[]{:S(2)}) collective-permute-start(f32[3,12,2,132]{3,2,1,0:T(2,128)S(1)} %get-tuple-element.183), channel_id=1, source_target_pairs={{0,1},{2,3},{4,5},{6,7},{8,9},{10,11},{12,13},{14,15},{16,17},{18,... | collective-permute-start | bytes 114056 | tf_op jit(solution)/shard_map/ppermute | solution.py:26
  169.3 3.9 %collective-permute-start.17 = (f32[3,12,2,132]{3,2,1,0:T(2,128)S(1)}, f32[3,12,2,132]{3,2,1,0:T(2,128)S(1)}, u32[]{:S(2)}, u32[]{:S(2)}) collective-permute-start(f32[3,12,2,132]{3,2,1,0:T(2,128)S(1)} %get-tuple-element.184), channel_id=1, source_target_pairs={{1,0},{3,2},{5,4},{7,6},{9,8},{11,10},{13,12},{15,14},{17,16},{19,... | collective-permute-start | bytes 114056 | tf_op jit(solution)/shard_map/ppermute | solution.py:27
where the time goes:
time: 182 us; the launch traced here: 181 us
  waiting for transfers between devices  84.4 us (46%)
  starting transfers between devices  68.9 us (38%)
  other arithmetic  23.5 us (13%)
  local copies, waits for them, and re-layouts  2.65 us (1%)
    ppermute x9, waiting for transfers between devices, padded(): after = lax.ppermute(leading, axis, down)  59.6 us
    ppermute x9, starting transfers between devices, padded(): before = lax.ppermute(last, axis, up)  38 us
    ppermute x9, starting transfers between devices, padded(): after = lax.ppermute(leading, axis, down)  30.9 us
    ppermute x9, waiting for transfers between devices, padded(): before = lax.ppermute(last, axis, up)  24.7 us
    another operation x12, other arithmetic, sweep(): return (jnp.stack(force_parts), jnp.stack(turned_parts), sensitivity)  9.05 us
    add x1, other arithmetic, shards(): grad_modulus = sens_moved + sens_start  5.34 us
  transfers between devices with their start and end apart: 18, of which 14 were waited for; matrix products, arithmetic and copies ran while one was open for 0% of the time, Pallas kernels for 0%

commit v1 on v0

v1 whole, which is shorter than its diff:
```python
import math

import jax
import jax.numpy as jnp
from jax import lax
from jax.experimental import pallas as pl
from jax.experimental.pallas import tpu as pltpu
from jax.sharding import PartitionSpec as P

BOND_OFFSETS = [
    (p, q, r)
    for p in range(-2, 3)
    for q in range(-2, 3)
    for r in range(-2, 3)
    if 0 < p * p + q * q + r * r <= 4
]
F32 = jnp.float32
NPL, NROW, NLANE = 8, 16, 128
DISP, CARRIED, MOVED, BACK = range(4)
SETS = 4
MESH = pl.DeviceIdType.MESH
NEIGHBOURS = [
    (da, dr, dd)
    for dd in (0, 1)
    for dr in (-1, 0, 1)
    for da in (-1, 0, 1)
    if (da, dr, dd) != (0, 0, 0)
]
MESSAGES = sorted(NEIGHBOURS, key=lambda n: (not (n[0] == 0 and n[2] == 0), abs(n[1])))
NEAR = [n for n in MESSAGES if n[1] == 0]
RADIAL = {
    side: [n for n in MESSAGES if n[1] == (-1 if side else 1)] for side in (0, 1)
}


def size_of(offset):
    length_sq = sum(o * o for o in offset)
    mult = max(abs(o) for o in offset)
    return mult, 2.0 * mult / length_sq, mult / math.sqrt(length_sq)


def signed(offset, parts):
    total = None
    for o, part in zip(offset, parts):
        if o != 0:
            if total is None:
                total = part if o > 0 else -part
            else:
                total = total + part if o > 0 else total - part
    return total


def add_signed(offset, parts, value):
    return [
        part if o == 0 else (part + value if o > 0 else part - value)
        for o, part in zip(offset, parts)
    ]


def kernel(
    disp_h,
    vel_h,
    mod_h,
    cls_h,
    bi_h,
    dens,
    adjd_h,
    adjv_h,
    moved_h,
    newv_h,
    gdisp_h,
    gvel_h,
    gmod_h,
    disp,
    vel,
    mod,
    cls,
    bi,
    adjd,
    adjv,
    rden,
    w,
    m,
    ecoef,
    gcoef,
    acoef,
    bcoef,
    xcoef,
    force1,
    force2,
    turn2,
    turn3,
    sens,
    o_newv,
    o_gvel,
    o_gdisp,
    o_gmod,
    pack,
    sd,
    se,
    sf,
    rp,
    rpr,
    rd,
    rf,
    rdr,
    re,
    rer,
    load_sem,
    store_sem,
    send_sem,
    recv_sem,
):
    az, rad, dep = lax.axis_index("az"), lax.axis_index("rad"), lax.axis_index("dep")
    naz, nrad = lax.axis_size("az"), lax.axis_size("rad")
    lane = lax.broadcasted_iota(jnp.int32, (NROW, NLANE), 1)
    lane8 = lax.broadcasted_iota(jnp.int32, (8, NLANE), 1)
    sub8 = lax.broadcasted_iota(jnp.int32, (8, NLANE), 0)

    def place(n):
        da, dr, dd = n
        return {
            "az": lax.rem(az + (da + naz), naz),
            "rad": lax.rem(rad + (dr + nrad), nrad),
            "dep": (1 - dep) if dd else dep,
        }

    barrier = pltpu.get_barrier_semaphore()
    for n in NEIGHBOURS:
        pl.semaphore_signal(barrier, inc=1, device_id=place(n), device_id_type=MESH)

    loads = {}
    for j, (name, src, dst) in enumerate(
        (
            ("disp", disp_h, disp),
            ("mod", mod_h, mod),
            ("cls", cls_h, cls),
            ("adjv", adjv_h, adjv),
            ("bi", bi_h, bi),
            ("vel", vel_h, vel),
            ("adjd", adjd_h, adjd),
        )
    ):
        loads[name] = pltpu.make_async_copy(src, dst, load_sem.at[j])
        loads[name].start()

    edge_row = 15 - 15 * dep
    second_row = 14 - 13 * dep
    halo_row = 8 + 16 - 17 * dep
    halo_row2 = 8 + 17 - 19 * dep
    blank = 24 * dep
    blank = pl.multiple_of(24 - 24 * (1 - dep), 8)

    def clear(ref):
        ref[:, pl.ds(blank, 8), :] = jnp.zeros((12, 8, NLANE), F32)
        for plane in (0, 1, 10, 11):
            ref[plane] = jnp.zeros((32, NLANE), F32)

    def clear_w(j, carry):
        clear(w.at[j])
        return carry

    def clear_m(j, carry):
        clear(m.at[j])
        return carry

    lax.fori_loop(0, SETS * 9, clear_w, 0)
    lax.fori_loop(0, 5, clear_m, 0)
    sd[...] = jnp.zeros(sd.shape, F32)
    pack[...] = jnp.zeros(pack.shape, F32)

    def chan(t, c, r):
        return w.at[t * 9 + c * 3 + 1 + r]

    def near(t, c, offset, i):
        p, q, r = offset
        if abs(r) == 2:
            return w[SETS * 9 + t * 2 + (r > 0), i + 2, 8:24, :]
        return w[t * 9 + c * 3 + 1 + r, i + (2 + p), 8 + q : 24 + q, :]

    def near_m(offset, i):
        p, q, r = offset
        return m[2 + r, i + (2 + p), 8 + q : 24 + q, :]

    def centre(t, i):
        return [w[t * 9 + c * 3 + 1, i + 2, 8:24, :] for c in range(3)]

    def project(t, offset, i, cen):
        parts = [near(t, c, offset, i) if offset[c] else None for c in range(3)]
        return signed(offset, parts) - signed(offset, cen)

    def pack_plane(t, i, with_mod):
        packed = pack[t]
        for c in range(4 if with_mod else 3):
            ref = m.at[2] if c == 3 else chan(t, c, 0)
            group = 4 * i + c
            rolled = pltpu.roll(ref[i + 2, 8:24, :], 4 * group + 2, 1)
            packed = jnp.where(lane // 4 == group, rolled, packed)
            sd[t, i, c : c + 1, :] = ref[i + 2, pl.ds(8 + edge_row, 1), :]
            if c in (1, 3):
                at = 4 if c == 1 else 5
                sd[t, i, at : at + 1, :] = ref[i + 2, pl.ds(8 + second_row, 1), :]
        pack[t] = packed

    def pack_faces(t, with_mod):
        packed = pack[t]
        for side in (0, 1):
            outer, inner = (9, 8) if side else (2, 3)
            for c in range(3):
                sf[side, t, c] = chan(t, c, 0)[outer, 8:24, :]
            sf[side, t, 3] = chan(t, 0, 0)[inner, 8:24, :]
            if with_mod:
                sf[side, t, 4] = m[2, outer, 8:24, :]
                sf[side, t, 5] = m[2, inner, 8:24, :]
            turned = pltpu.roll(packed, 16, 1) if side else packed
            for half in (0, 1):
                y = jnp.where(lane8 < 16, turned[8 * half : 8 * half + 8], 0.0)
                for bit in (1, 2, 4):
                    y = jnp.where((sub8 & bit) != 0, pltpu.roll(y, 16 * bit, 1), y)
                se[side, t, half : half + 1, :] = jnp.sum(y, axis=0, keepdims=True)

    def copies(phase):
        made = {}
        first, count = ((0, 2), (2, 1), (3, 1))[phase]
        sets = pl.ds(first, count)
        for j, n in enumerate(MESSAGES):
            da, dr, dd = n
            a = 0 if da == 1 else 1
            out = 1 if dr == 1 else 0
            r = 1 - out
            if da == 0 and dd == 0:
                planes = pl.ds(0, 6 if phase == 0 else 4)
                pair = sf.at[out, first, planes], rf.at[r, first, planes]
            elif da == 0 and dr == 0:
                pair = sd.at[sets], rd.at[sets]
            elif da == 0:
                plane = 7 if dr == 1 else 0
                rows = pl.ds(0, 4)
                pair = sd.at[sets, plane, rows], rdr.at[r, sets, rows]
            elif dr == 0 and dd == 0:
                pair = pack.at[sets], rp.at[a, sets]
            elif dr == 0:
                pair = pack.at[sets, pl.ds(edge_row, 1)], rpr.at[a, sets]
            elif dd == 0:
                pair = se.at[out, sets], re.at[a, r, sets]
            else:
                pair = se.at[out, sets, pl.ds(1 - dep, 1)], rer.at[a, r, sets]
            made[n] = pltpu.make_async_remote_copy(
                src_ref=pair[0],
                dst_ref=pair[1],
                send_sem=send_sem.at[phase * 17 + j],
                recv_sem=recv_sem.at[phase * 17 + j],
                device_id=place(n),
                device_id_type=MESH,
            )
        return made

    def carried_copies():
        made = {}
        for out in (0, 1):
            made[1 - out] = pltpu.make_async_remote_copy(
                src_ref=sf.at[out, CARRIED, pl.ds(0, 4)],
                dst_ref=rf.at[1 - out, CARRIED, pl.ds(0, 4)],
                send_sem=send_sem.at[51 + out],
                recv_sem=recv_sem.at[51 + out],
                device_id=place((0, 1 if out else -1, 0)),
                device_id_type=MESH,
            )
        return made

    def both(left, right, lanes):
        return jnp.where(lanes % 4 < 2, left, right)

    def shifted(value, edge, lanes, by):
        if by > 0:
            return pltpu.roll(jnp.where(lanes < by, edge, value), NLANE - by, 1)
        return pltpu.roll(jnp.where(lanes >= NLANE + by, edge, value), -by, 1)

    def spread(row, step, bits):
        y = jnp.broadcast_to(row, (8, NLANE))
        for bit in bits:
            turned = pltpu.roll(y, (NLANE - step * bit) % NLANE, 1)
            y = jnp.where((sub8 & bit) != 0, turned, y)
        return y

    def turn_left(value, by):
        return pltpu.roll(value, lax.rem(2 * NLANE - by, NLANE), 1)

    def take_own(t, with_mod):
        sides = both(rp[0, t], rp[1, t], lane)
        rows = spread(both(rpr[0, t], rpr[1, t], lane8[0:1]), 4, (1, 2))

        def plane(i, carry):
            for c in range(4 if with_mod else 3):
                ref = m.at[2] if c == 3 else chan(t, c, 0)
                value = ref[i + 2, 8:24, :]
                edge = turn_left(sides, 16 * i + (4 * c + 2))
                for r in (-1, 1):
                    to = m.at[2 + r] if c == 3 else chan(t, c, r)
                    to[i + 2, 8:24, :] = shifted(value, edge, lane, r)
                if c >= 2:
                    for r in (-2, 2):
                        to = m.at[2 + r] if c == 3 else w.at[SETS * 9 + t * 2 + (r > 0)]
                        to[i + 2, 8:24, :] = shifted(value, edge, lane, r)
            tile = rd[t, i]
            edge = turn_left(rows, 16 * i + 2)
            for r in (-1, 0, 1):
                moved = tile if r == 0 else shifted(tile, edge, lane8, r)
                for c in range(4 if with_mod else 3):
                    to = m.at[2 + r] if c == 3 else chan(t, c, r)
                    to[i + 2, pl.ds(halo_row, 1), :] = moved[c : c + 1]
            chan(t, 1, 0)[i + 2, pl.ds(halo_row2, 1), :] = tile[4:5]
            if with_mod:
                m[2, i + 2, pl.ds(halo_row2, 1), :] = tile[5:6]
            return carry

        lax.fori_loop(0, NPL, plane, 0)

    def take_radial(t, side, with_mod):
        at, far = (10, 11) if side else (1, 0)
        there = (rad < nrad - 1) if side else (rad > 0)
        present = jnp.where(there, 1.0, 0.0).astype(F32)
        edges = [
            spread(
                both(
                    re[0, side, t, h : h + 1, :], re[1, side, t, h : h + 1, :], lane8[0:1]
                ),
                16,
                (1, 2, 4),
            )
            for h in (0, 1)
        ]
        for c in range(4 if with_mod else 3):
            value = rf[side, t, 4 if c == 3 else c]
            turned = [pltpu.roll(e, NLANE - (4 * c + 2), 1) for e in edges]
            edge = jnp.concatenate(turned, axis=0)
            for r in (-1, 0, 1):
                new = value if r == 0 else shifted(value, edge, lane, r)
                if c == 3:
                    m[2 + r, at, 8:24, :] = new * present
                else:
                    chan(t, c, r)[at, 8:24, :] = new
        chan(t, 0, 0)[far, 8:24, :] = rf[side, t, 3]
        if with_mod:
            m[2, far, 8:24, :] = rf[side, t, 5] * present
        rows = spread(both(rer[0, side, t], rer[1, side, t], lane8[0:1]), 4, (1, 2))
        edge = turn_left(rows, 16 * 7 * dep + 2)
        tile = rdr[side, t]
        for r in (-1, 0, 1):
            moved = tile if r == 0 else shifted(tile, edge, lane8, r)
            for c in range(4 if with_mod else 3):
                if c == 3:
                    m[2 + r, at, pl.ds(halo_row, 1), :] = moved[3:4] * present
                else:
                    chan(t, c, r)[at, pl.ds(halo_row, 1), :] = moved[c : c + 1]

    def bond_first(offset, i, cen, cm, intact, forces):
        mult, kappa, scale = size_of(offset)
        nm = near_m(offset, i)
        half = cm * nm / (cm + nm)
        e = intact * half * scale
        bend = jnp.tanh(kappa * project(DISP, offset, i, cen))
        push = e * bend
        g = e * half
        return add_signed(offset, forces, push), (
            e,
            g,
            kappa * (e - push * bend),
            g * bend,
        )

    def bond_second(offset, i, cen, cen_z, e, g, forces, turns, total):
        kappa = size_of(offset)[1]
        bend = jnp.tanh(kappa * project(MOVED, offset, i, cen))
        pull = project(CARRIED, offset, i, cen_z)
        push = e * bend
        stiff = kappa * (e - push * bend) * pull
        forces = add_signed(offset, forces, push)
        turns = add_signed(offset, turns, stiff)
        return forces, turns, total + g * bend * pull

    def bond_third(offset, i, cen_z, a, b, turns, total):
        pull = project(BACK, offset, i, cen_z)
        return add_signed(offset, turns, a * pull), total + b * pull

    def zeros(count):
        return [jnp.zeros((NROW, NLANE), F32) for _ in range(count)]

    def crossing(side):
        sign = 1 if side else -1
        outer, inner = (7, 6) if side else (0, 1)
        found = [(outer, k) for k, o in enumerate(BOND_OFFSETS) if o[0] == sign]
        double = BOND_OFFSETS.index((2 * sign, 0, 0))
        return found + [(outer, double), (inner, double)]

    def cross_first(side):
        for j, (i, k) in enumerate(crossing(side)):
            offset = BOND_OFFSETS[k]
            forces = [force1[c, i] for c in range(3)]
            forces, made = bond_first(
                offset, i, centre(DISP, i), m[2, i + 2, 8:24, :], bi[k, i], forces
            )
            for c in range(3):
                if offset[c]:
                    force1[c, i] = forces[c]
            for n, value in enumerate(made):
                xcoef[n, side * 11 + j] = value

    def cross_second(side):
        for j, (i, k) in enumerate(crossing(side)):
            offset = BOND_OFFSETS[k]
            x = side * 11 + j
            forces, turns, total = bond_second(
                offset,
                i,
                centre(MOVED, i),
                centre(CARRIED, i),
                xcoef[0, x],
                xcoef[1, x],
                [force2[c, i] for c in range(3)],
                [turn2[c, i] for c in range(3)],
                sens[i],
            )
            for c in range(3):
                if offset[c]:
                    force2[c, i] = forces[c]
                    turn2[c, i] = turns[c]
            sens[i] = total

    def cross_third(side):
        for j, (i, k) in enumerate(crossing(side)):
            offset = BOND_OFFSETS[k]
            x = side * 11 + j
            turns, total = bond_third(
                offset,
                i,
                centre(BACK, i),
                xcoef[2, x],
                xcoef[3, x],
                [turn3[c, i] for c in range(3)],
                sens[i],
            )
            for c in range(3):
                if offset[c]:
                    turn3[c, i] = turns[c]
            sens[i] = total

    for name in ("disp", "mod", "cls", "adjv"):
        loads[name].wait()

    def begin(i, carry):
        kinds = cls[i]
        density = jnp.zeros((NROW, NLANE), F32)
        for level in range(8):
            density = jnp.where(kinds == level, dens[level], density)
        inverse = 1.0 / density
        rden[i] = inverse
        m[2, i + 2, 8:24, :] = mod[i]
        for c in range(3):
            chan(DISP, c, 0)[i + 2, 8:24, :] = disp[c, i]
            chan(CARRIED, c, 0)[i + 2, 8:24, :] = 0.25 * adjv[c, i] * inverse
        pack_plane(DISP, i, True)
        pack_plane(CARRIED, i, False)
        return carry

    lax.fori_loop(0, NPL, begin, 0)
    pack_faces(DISP, True)
    pack_faces(CARRIED, False)
    pl.semaphore_wait(barrier, len(NEIGHBOURS))
    sent = copies(0)
    for n in MESSAGES:
        sent[n].start()
    sent_carried = carried_copies()
    for side in (0, 1):
        sent_carried[side].start()
    for name in ("bi", "vel", "adjd"):
        loads[name].wait()
    for n in NEAR:
        sent[n].wait_recv()
    take_own(DISP, True)
    take_own(CARRIED, False)

    def sweep_first(i, carry):
        cen, cm, forces = centre(DISP, i), m[2, i + 2, 8:24, :], zeros(3)
        for k, offset in enumerate(BOND_OFFSETS):
            forces, made = bond_first(offset, i, cen, cm, bi[k, i], forces)
            for ref, value in zip((ecoef, gcoef, acoef, bcoef), made):
                ref[k, i] = value
        for c in range(3):
            force1[c, i] = forces[c]
        return carry

    lax.fori_loop(0, NPL, sweep_first, 0)

    def end_first(i):
        for c in range(3):
            accel = force1[c, i] * rden[i]
            moved = disp[c, i] + 0.5 * vel[c, i] + 0.125 * accel
            chan(MOVED, c, 0)[i + 2, 8:24, :] = moved
        pack_plane(MOVED, i, False)

    def inner_planes(step):
        def body(j, carry):
            step(j + 2)
            return carry

        lax.fori_loop(0, 4, body, 0)

    def outer_planes(step):
        def body(j, carry):
            step(j + 4 * (j // 2))
            return carry

        lax.fori_loop(0, 4, body, 0)

    inner_planes(end_first)
    for n in MESSAGES:
        sent[n].wait_send()
    for side in (0, 1):
        for n in RADIAL[side]:
            sent[n].wait_recv()
        take_radial(DISP, side, True)
        cross_first(side)
    outer_planes(end_first)
    pack_faces(MOVED, False)

    sent = copies(1)
    for n in MESSAGES:
        sent[n].start()
    moved_out = [
        pltpu.make_async_copy(
            chan(MOVED, c, 0).at[pl.ds(2, NPL), pl.ds(8, NROW)], moved_h.at[c], store_sem.at[c]
        )
        for c in range(3)
    ]
    for copy in moved_out:
        copy.start()
    for side in (0, 1):
        sent_carried[side].wait_recv()
        sent_carried[side].wait_send()
        take_radial(CARRIED, side, False)
    for n in NEAR:
        sent[n].wait_recv()
    take_own(MOVED, False)

    def sweep_second(i, carry):
        cen, cen_z = centre(MOVED, i), centre(CARRIED, i)
        forces, turns, total = zeros(3), zeros(3), zeros(1)[0]
        for k, offset in enumerate(BOND_OFFSETS):
            forces, turns, total = bond_second(
                offset, i, cen, cen_z, ecoef[k, i], gcoef[k, i], forces, turns, total
            )
        for c in range(3):
            force2[c, i] = forces[c]
            turn2[c, i] = turns[c]
        sens[i] = total
        return carry

    lax.fori_loop(0, NPL, sweep_second, 0)

    def end_second(i):
        for c in range(3):
            total = adjd[c, i] + turn2[c, i]
            turn2[c, i] = total
            back = (0.25 * adjv[c, i] + 0.125 * total) * rden[i]
            chan(BACK, c, 0)[i + 2, 8:24, :] = back
        pack_plane(BACK, i, False)

    inner_planes(end_second)
    for n in MESSAGES:
        sent[n].wait_send()
    for side in (0, 1):
        for n in RADIAL[side]:
            sent[n].wait_recv()
        take_radial(MOVED, side, False)
        cross_second(side)
    outer_planes(end_second)
    pack_faces(BACK, False)

    sent = copies(2)
    for n in MESSAGES:
        sent[n].start()

    def velocities(i, carry):
        for c in range(3):
            accel = (force1[c, i] + force2[c, i]) * rden[i]
            o_newv[c, i] = vel[c, i] + 0.25 * accel
            o_gvel[c, i] = adjv[c, i] + 0.5 * turn2[c, i]
        return carry

    lax.fori_loop(0, NPL, velocities, 0)
    outs = [
        pltpu.make_async_copy(o_newv, newv_h, store_sem.at[3]),
        pltpu.make_async_copy(o_gvel, gvel_h, store_sem.at[4]),
    ]
    for copy in outs:
        copy.start()
    for n in NEAR:
        sent[n].wait_recv()
    take_own(BACK, False)

    def sweep_third(i, carry):
        cen_z, turns, total = centre(BACK, i), zeros(3), sens[i]
        for k, offset in enumerate(BOND_OFFSETS):
            turns, total = bond_third(offset, i, cen_z, acoef[k, i], bcoef[k, i], turns, total)
        for c in range(3):
            turn3[c, i] = turns[c]
        sens[i] = total
        return carry

    lax.fori_loop(0, NPL, sweep_third, 0)
    for n in MESSAGES:
        sent[n].wait_send()
    for side in (0, 1):
        for n in RADIAL[side]:
            sent[n].wait_recv()
        take_radial(BACK, side, False)
        cross_third(side)

    def finish(i, carry):
        for c in range(3):
            o_gdisp[c, i] = turn2[c, i] + turn3[c, i]
        o_gmod[i] = -sens[i] / (mod[i] * mod[i])
        return carry

    lax.fori_loop(0, NPL, finish, 0)
    last = [
        pltpu.make_async_copy(o_gdisp, gdisp_h, store_sem.at[5]),
        pltpu.make_async_copy(o_gmod, gmod_h, store_sem.at[6]),
    ]
    for copy in last:
        copy.start()
    for copy in moved_out + outs + last:
        copy.wait()


def shards(
    displacement, velocity, modulus, classes, bond_integrity, densities, adjoint_disp, adjoint_vel
):
    block = (NPL, NROW, NLANE)
    field = (3,) + block
    shape = jax.ShapeDtypeStruct
    vmem = pltpu.VMEM
    anywhere = pl.BlockSpec(memory_space=pl.ANY)
    scratch = [
        vmem(field, F32),
        vmem(field, F32),
        vmem(block, F32),
        vmem(block, jnp.int32),
        vmem((32,) + block, F32),
        vmem(field, F32),
        vmem(field, F32),
        vmem(block, F32),
        vmem((SETS * 11, 12, 32, NLANE), F32),
        vmem((5, 12, 32, NLANE), F32),
        vmem((32,) + block, F32),
        vmem((32,) + block, F32),
        vmem((32,) + block, F32),
        vmem((32,) + block, F32),
        vmem((4, 22, NROW, NLANE), F32),
        vmem(field, F32),
        vmem(field, F32),
        vmem(field, F32),
        vmem(field, F32),
        vmem(block, F32),
        vmem(field, F32),
        vmem(field, F32),
        vmem(field, F32),
        vmem(block, F32),
        vmem((SETS, NROW, NLANE), F32),
        vmem((SETS, NPL, 8, NLANE), F32),
        vmem((2, SETS, 2, NLANE), F32),
        vmem((2, SETS, 6, NROW, NLANE), F32),
        vmem((2, SETS, NROW, NLANE), F32),
        vmem((2, SETS, 1, NLANE), F32),
        vmem((SETS, NPL, 8, NLANE), F32),
        vmem((2, SETS, 6, NROW, NLANE), F32),
        vmem((2, SETS, 8, NLANE), F32),
        vmem((2, 2, SETS, 2, NLANE), F32),
        vmem((2, 2, SETS, 1, NLANE), F32),
        pltpu.SemaphoreType.DMA((7,)),
        pltpu.SemaphoreType.DMA((7,)),
        pltpu.SemaphoreType.DMA((53,)),
        pltpu.SemaphoreType.DMA((53,)),
    ]
    return pl.pallas_call(
        kernel,
        out_shape=(
            shape(field, F32),
            shape(field, F32),
            shape(field, F32),
            shape(field, F32),
            shape(block, F32),
        ),
        in_specs=[anywhere] * 5 + [pl.BlockSpec(memory_space=pltpu.SMEM)] + [anywhere] * 2,
        out_specs=[anywhere] * 5,
        scratch_shapes=scratch,
        compiler_params=pltpu.CompilerParams(
            collective_id=0, has_side_effects=True, vmem_limit_bytes=48 * 1024 * 1024
        ),
        name="rock_wall_step",
    )(
        displacement,
        velocity,
        modulus,
        classes,
        bond_integrity,
        densities,
        adjoint_disp,
        adjoint_vel,
    )


def solution(mesh):
    field = P(None, "rad", "dep", "az")
    block = P("rad", "dep", "az")
    return jax.shard_map(
        shards,
        mesh=mesh,
        in_specs=(field, field, block, block, field, P(), field, field),
        out_specs=(field, field, field, field, block),
        check_vma=False,
    )
```

time: 182 us -> 69.3 us (0.38)
  the two profiles are of different devices: /device:TPU:41 before, /device:TPU:1 now
where the time goes in v1:
time: 69.3 us; the launch traced here: 68.9 us
  Pallas kernels  57.3 us (83%)
  local copies, waits for them, and re-layouts  11 us (16%)
    pallas_call x1, Pallas kernels, shards(): pl.pallas_call(kernel, out_shape=(shape(field, F32), shape(field, F32), s...  57.3 us
    unnamed x21, local copies, waits for them, and re-layouts  11 us

profile of v1, /device:TPU:1, one launch (start us, length us, event | category | flops | bytes accessed | tf_op | source)
XLA Modules:
  0.0 68.9 jit_solution(16982753106995902462)
XLA Ops:
  0.6 0.0 copy-start
  0.6 1.6 %copy-done = f32[32,8,16,128]{3,2,1,0:T(8,128)S(1)} copy-done((f32[32,8,16,128]{3,2,1,0:T(8,128)S(1)}, f32[32,8,16,128]{3,2,1,0:T(8,128)}, u32[]{:S(2)}) %copy-start) | copy-done | bytes 2097176
  2.2 0.0 copy-start.1
  2.2 0.9 %copy-done.1 = f32[3,8,16,128]{3,2,1,0:T(8,128)S(1)} copy-done((f32[3,8,16,128]{3,2,1,0:T(8,128)S(1)}, f32[3,8,16,128]{3,2,1,0:T(8,128)}, u32[]{:S(2)}) %copy-start.1) | copy-done | bytes 196632
  3.2 0.0 copy-start.2
  3.2 0.9 %copy-done.2 = f32[3,8,16,128]{3,2,1,0:T(8,128)S(1)} copy-done((f32[3,8,16,128]{3,2,1,0:T(8,128)S(1)}, f32[3,8,16,128]{3,2,1,0:T(8,128)}, u32[]{:S(2)}) %copy-start.2) | copy-done | bytes 196632
  4.1 0.0 copy-start.3
  4.1 0.9 %copy-done.3 = f32[3,8,16,128]{3,2,1,0:T(8,128)S(1)} copy-done((f32[3,8,16,128]{3,2,1,0:T(8,128)S(1)}, f32[3,8,16,128]{3,2,1,0:T(8,128)}, u32[]{:S(2)}) %copy-start.3) | copy-done | bytes 196632
  5.0 0.0 copy-start.4
  5.0 0.9 %copy-done.4 = f32[3,8,16,128]{3,2,1,0:T(8,128)S(1)} copy-done((f32[3,8,16,128]{3,2,1,0:T(8,128)S(1)}, f32[3,8,16,128]{3,2,1,0:T(8,128)}, u32[]{:S(2)}) %copy-start.4) | copy-done | bytes 196632
  5.9 0.0 copy-start.5
  5.9 0.8 %copy-done.5 = f32[8,16,128]{2,1,0:T(8,128)S(1)} copy-done((f32[8,16,128]{2,1,0:T(8,128)S(1)}, f32[8,16,128]{2,1,0:T(8,128)}, u32[]{:S(2)}) %copy-start.5) | copy-done | bytes 65560
  6.8 0.0 copy-start.6
  6.8 0.8 %copy-done.6 = s32[8,16,128]{2,1,0:T(8,128)S(1)} copy-done((s32[8,16,128]{2,1,0:T(8,128)S(1)}, s32[8,16,128]{2,1,0:T(8,128)}, u32[]{:S(2)}) %copy-start.6) | copy-done | bytes 65560
  7.6 0.0 copy-start.7
  7.6 0.7 copy-done.7
  8.3 57.3 %rock_wall_step.1 = (f32[3,8,16,128]{3,2,1,0:T(8,128)S(1)}, f32[3,8,16,128]{3,2,1,0:T(8,128)S(1)}, f32[3,8,16,128]{3,2,1,0:T(8,128)S(1)}, f32[3,8,16,128]{3,2,1,0:T(8,128)S(1)}, f32[8,16,128]{2,1,0:T(8,128)S(1)}) custom-call(f32[3,8,16,128]{3,2,1,0:T(8,128)S(1)} %copy-done.1, f32[3,8,16,128]{3,2,1,0:T(8,128)S(1)} %copy-done.2, f32[8,16,128]{2,1,0:T(8,128)S(1)} %copy-done.5, ...), custom_call_target="tpu_custom_call" | custom-call | tf_op jit(solution)/shard_map/rock_wall_step/pallas_call | solution.py:686
  65.6 0.7 copy.18
  66.2 0.7 copy.19
  66.9 0.7 copy.20
  67.6 0.7 copy.21
  68.3 0.6 copy.22
Async XLA Ops:
  0.6 1.6 %copy-start = (f32[32,8,16,128]{3,2,1,0:T(8,128)S(1)}, f32[32,8,16,128]{3,2,1,0:T(8,128)}, u32[]{:S(2)}) copy-start(f32[32,8,16,128]{3,2,1,0:T(8,128)} %bi_h.1) | copy-start | bytes 6291460
  2.2 0.9 %copy-start.1 = (f32[3,8,16,128]{3,2,1,0:T(8,128)S(1)}, f32[3,8,16,128]{3,2,1,0:T(8,128)}, u32[]{:S(2)}) copy-start(f32[3,8,16,128]{3,2,1,0:T(8,128)} %disp_h.1) | copy-start | bytes 589828
  3.2 0.9 %copy-start.2 = (f32[3,8,16,128]{3,2,1,0:T(8,128)S(1)}, f32[3,8,16,128]{3,2,1,0:T(8,128)}, u32[]{:S(2)}) copy-start(f32[3,8,16,128]{3,2,1,0:T(8,128)} %vel_h.1) | copy-start | bytes 589828
  4.1 0.9 %copy-start.3 = (f32[3,8,16,128]{3,2,1,0:T(8,128)S(1)}, f32[3,8,16,128]{3,2,1,0:T(8,128)}, u32[]{:S(2)}) copy-start(f32[3,8,16,128]{3,2,1,0:T(8,128)} %adjd_h.1) | copy-start | bytes 589828
  5.0 0.9 %copy-start.4 = (f32[3,8,16,128]{3,2,1,0:T(8,128)S(1)}, f32[3,8,16,128]{3,2,1,0:T(8,128)}, u32[]{:S(2)}) copy-start(f32[3,8,16,128]{3,2,1,0:T(8,128)} %adjv_h.1) | copy-start | bytes 589828
  5.9 0.8 %copy-start.5 = (f32[8,16,128]{2,1,0:T(8,128)S(1)}, f32[8,16,128]{2,1,0:T(8,128)}, u32[]{:S(2)}) copy-start(f32[8,16,128]{2,1,0:T(8,128)} %mod_h.1) | copy-start | bytes 196612
  6.8 0.8 %copy-start.6 = (s32[8,16,128]{2,1,0:T(8,128)S(1)}, s32[8,16,128]{2,1,0:T(8,128)}, u32[]{:S(2)}) copy-start(s32[8,16,128]{2,1,0:T(8,128)} %cls_h.1) | copy-start | bytes 196612
  7.6 0.7 copy-start.7

commit v2 on v1

--- a/solution.py
+++ b/solution.py
@@ -114,6 +114,8 @@
     az, rad, dep = lax.axis_index("az"), lax.axis_index("rad"), lax.axis_index("dep")
     naz, nrad = lax.axis_size("az"), lax.axis_size("rad")
     lane = lax.broadcasted_iota(jnp.int32, (NROW, NLANE), 1)
+    lane_all = lax.broadcasted_iota(jnp.int32, (NPL, NROW, NLANE), 2)
+    lane8_all = lax.broadcasted_iota(jnp.int32, (NPL, 8, NLANE), 2)
     lane8 = lax.broadcasted_iota(jnp.int32, (8, NLANE), 1)
     sub8 = lax.broadcasted_iota(jnp.int32, (8, NLANE), 0)
 
@@ -148,8 +150,7 @@
     second_row = 14 - 13 * dep
     halo_row = 8 + 16 - 17 * dep
     halo_row2 = 8 + 17 - 19 * dep
-    blank = 24 * dep
-    blank = pl.multiple_of(24 - 24 * (1 - dep), 8)
+    blank = pl.multiple_of(24 * dep, 8)
 
     def clear(ref):
         ref[:, pl.ds(blank, 8), :] = jnp.zeros((12, 8, NLANE), F32)
@@ -189,21 +190,27 @@
         parts = [near(t, c, offset, i) if offset[c] else None for c in range(3)]
         return signed(offset, parts) - signed(offset, cen)
 
-    def pack_plane(t, i, with_mod):
-        packed = pack[t]
+    def pack_planes(t, first, count, with_mod):
+        at = pl.ds(2 + first, count)
+        here = pl.ds(first, count)
+        groups = None
+        lanes = lane_all[:count]
         for c in range(4 if with_mod else 3):
             ref = m.at[2] if c == 3 else chan(t, c, 0)
-            group = 4 * i + c
-            rolled = pltpu.roll(ref[i + 2, 8:24, :], 4 * group + 2, 1)
-            packed = jnp.where(lane // 4 == group, rolled, packed)
-            sd[t, i, c : c + 1, :] = ref[i + 2, pl.ds(8 + edge_row, 1), :]
+            rolled = pltpu.roll(ref[at, 8:24, :], 4 * c + 2, 2)
+            groups = rolled if c == 0 else jnp.where(lanes >= 4 * c, rolled, groups)
+            sd[t, here, c : c + 1, :] = ref[at, pl.ds(8 + edge_row, 1), :]
             if c in (1, 3):
-                at = 4 if c == 1 else 5
-                sd[t, i, at : at + 1, :] = ref[i + 2, pl.ds(8 + second_row, 1), :]
+                row = 4 if c == 1 else 5
+                sd[t, here, row : row + 1, :] = ref[at, pl.ds(8 + second_row, 1), :]
+        packed = pack[t]
+        for j in range(count):
+            i = first + j
+            rolled = pltpu.roll(groups[j], 16 * i, 1) if i else groups[j]
+            packed = jnp.where(lane // 16 == i, rolled, packed)
         pack[t] = packed
 
     def pack_faces(t, with_mod):
-        packed = pack[t]
         for side in (0, 1):
             outer, inner = (9, 8) if side else (2, 3)
             for c in range(3):
@@ -212,6 +219,10 @@
             if with_mod:
                 sf[side, t, 4] = m[2, outer, 8:24, :]
                 sf[side, t, 5] = m[2, inner, 8:24, :]
+
+    def pack_corners(t):
+        packed = pack[t]
+        for side in (0, 1):
             turned = pltpu.roll(packed, 16, 1) if side else packed
             for half in (0, 1):
                 y = jnp.where(lane8 < 16, turned[8 * half : 8 * half + 8], 0.0)
@@ -272,9 +283,10 @@
         return jnp.where(lanes % 4 < 2, left, right)
 
     def shifted(value, edge, lanes, by):
+        last = value.ndim - 1
         if by > 0:
-            return pltpu.roll(jnp.where(lanes < by, edge, value), NLANE - by, 1)
-        return pltpu.roll(jnp.where(lanes >= NLANE + by, edge, value), -by, 1)
+            return pltpu.roll(jnp.where(lanes < by, edge, value), NLANE - by, last)
+        return pltpu.roll(jnp.where(lanes >= NLANE + by, edge, value), -by, last)
 
     def spread(row, step, bits):
         y = jnp.broadcast_to(row, (8, NLANE))
@@ -288,33 +300,33 @@
 
     def take_own(t, with_mod):
         sides = both(rp[0, t], rp[1, t], lane)
+        sides = jnp.stack(
+            [pltpu.roll(sides, NLANE - 16 * i, 1) if i else sides for i in range(NPL)]
+        )
         rows = spread(both(rpr[0, t], rpr[1, t], lane8[0:1]), 4, (1, 2))
-
-        def plane(i, carry):
+        rows = jnp.stack([pltpu.roll(rows, NLANE - 16 * i - 2, 1) for i in range(NPL)])
+        tile = rd[t]
+        own = pl.ds(2, NPL)
+        for c in range(4 if with_mod else 3):
+            ref = m.at[2] if c == 3 else chan(t, c, 0)
+            value = ref[own, 8:24, :]
+            edge = pltpu.roll(sides, NLANE - (4 * c + 2), 2)
+            for r in (-2, -1, 1, 2) if c >= 2 else (-1, 1):
+                if c == 3:
+                    to = m.at[2 + r]
+                elif abs(r) == 2:
+                    to = w.at[SETS * 9 + t * 2 + (r > 0)]
+                else:
+                    to = chan(t, c, r)
+                to[own, 8:24, :] = shifted(value, edge, lane_all, r)
+        for r in (-1, 0, 1):
+            moved = tile if r == 0 else shifted(tile, rows, lane8_all, r)
             for c in range(4 if with_mod else 3):
-                ref = m.at[2] if c == 3 else chan(t, c, 0)
-                value = ref[i + 2, 8:24, :]
-                edge = turn_left(sides, 16 * i + (4 * c + 2))
-                for r in (-1, 1):
-                    to = m.at[2 + r] if c == 3 else chan(t, c, r)
-                    to[i + 2, 8:24, :] = shifted(value, edge, lane, r)
-                if c >= 2:
-                    for r in (-2, 2):
-                        to = m.at[2 + r] if c == 3 else w.at[SETS * 9 + t * 2 + (r > 0)]
-                        to[i + 2, 8:24, :] = shifted(value, edge, lane, r)
-            tile = rd[t, i]
-            edge = turn_left(rows, 16 * i + 2)
-            for r in (-1, 0, 1):
-                moved = tile if r == 0 else shifted(tile, edge, lane8, r)
-                for c in range(4 if with_mod else 3):
-                    to = m.at[2 + r] if c == 3 else chan(t, c, r)
-                    to[i + 2, pl.ds(halo_row, 1), :] = moved[c : c + 1]
-            chan(t, 1, 0)[i + 2, pl.ds(halo_row2, 1), :] = tile[4:5]
-            if with_mod:
-                m[2, i + 2, pl.ds(halo_row2, 1), :] = tile[5:6]
-            return carry
-
-        lax.fori_loop(0, NPL, plane, 0)
+                to = m.at[2 + r] if c == 3 else chan(t, c, r)
+                to[own, pl.ds(halo_row, 1), :] = moved[:, c : c + 1]
+        chan(t, 1, 0)[own, pl.ds(halo_row2, 1), :] = tile[:, 4:5]
+        if with_mod:
+            m[2, own, pl.ds(halo_row2, 1), :] = tile[:, 5:6]
 
     def take_radial(t, side, with_mod):
         at, far = (10, 11) if side else (1, 0)
@@ -445,32 +457,34 @@
                     turn3[c, i] = turns[c]
             sens[i] = total
 
-    for name in ("disp", "mod", "cls", "adjv"):
-        loads[name].wait()
-
-    def begin(i, carry):
-        kinds = cls[i]
-        density = jnp.zeros((NROW, NLANE), F32)
-        for level in range(8):
-            density = jnp.where(kinds == level, dens[level], density)
-        inverse = 1.0 / density
-        rden[i] = inverse
-        m[2, i + 2, 8:24, :] = mod[i]
-        for c in range(3):
-            chan(DISP, c, 0)[i + 2, 8:24, :] = disp[c, i]
-            chan(CARRIED, c, 0)[i + 2, 8:24, :] = 0.25 * adjv[c, i] * inverse
-        pack_plane(DISP, i, True)
-        pack_plane(CARRIED, i, False)
-        return carry
-
-    lax.fori_loop(0, NPL, begin, 0)
+    own = pl.ds(2, NPL)
+    sent = copies(0)
+    sent_carried = carried_copies()
+    loads["disp"].wait()
+    loads["mod"].wait()
+    m[2, own, 8:24, :] = mod[...]
+    for c in range(3):
+        chan(DISP, c, 0)[own, 8:24, :] = disp[c]
     pack_faces(DISP, True)
+    pl.semaphore_wait(barrier, len(NEIGHBOURS))
+    for n in MESSAGES[:2]:
+        sent[n].start()
+    loads["cls"].wait()
+    loads["adjv"].wait()
+    kinds = cls[...]
+    density = jnp.full((NPL, NROW, NLANE), dens[0])
+    for level in range(1, 8):
+        density = jnp.where(kinds == level, dens[level], density)
+    rden[...] = 1.0 / density
+    for c in range(3):
+        chan(CARRIED, c, 0)[own, 8:24, :] = 0.25 * adjv[c] * rden[...]
+    pack_planes(DISP, 0, NPL, True)
+    pack_planes(CARRIED, 0, NPL, False)
+    pack_corners(DISP)
+    pack_corners(CARRIED)
     pack_faces(CARRIED, False)
-    pl.semaphore_wait(barrier, len(NEIGHBOURS))
-    sent = copies(0)
-    for n in MESSAGES:
+    for n in MESSAGES[2:]:
         sent[n].start()
-    sent_carried = carried_copies()
     for side in (0, 1):
         sent_carried[side].start()
     for name in ("bi", "vel", "adjd"):
@@ -492,28 +506,15 @@
 
     lax.fori_loop(0, NPL, sweep_first, 0)
 
-    def end_first(i):
+    def end_first(first, count):
+        here = pl.ds(first, count)
         for c in range(3):
-            accel = force1[c, i] * rden[i]
-            moved = disp[c, i] + 0.5 * vel[c, i] + 0.125 * accel
-            chan(MOVED, c, 0)[i + 2, 8:24, :] = moved
-        pack_plane(MOVED, i, False)
-
-    def inner_planes(step):
-        def body(j, carry):
-            step(j + 2)
-            return carry
-
-        lax.fori_loop(0, 4, body, 0)
-
-    def outer_planes(step):
-        def body(j, carry):
-            step(j + 4 * (j // 2))
-            return carry
-
-        lax.fori_loop(0, 4, body, 0)
-
-    inner_planes(end_first)
+            accel = force1[c, here] * rden[here]
+            moved = disp[c, here] + 0.5 * vel[c, here] + 0.125 * accel
+            chan(MOVED, c, 0)[pl.ds(2 + first, count), 8:24, :] = moved
+        pack_planes(MOVED, first, count, False)
+
+    end_first(2, 4)
     for n in MESSAGES:
         sent[n].wait_send()
     for side in (0, 1):
@@ -521,8 +522,10 @@
             sent[n].wait_recv()
         take_radial(DISP, side, True)
         cross_first(side)
-    outer_planes(end_first)
+    end_first(0, 2)
+    end_first(6, 2)
     pack_faces(MOVED, False)
+    pack_corners(MOVED)
 
     sent = copies(1)
     for n in MESSAGES:
@@ -558,15 +561,16 @@
 
     lax.fori_loop(0, NPL, sweep_second, 0)
 
-    def end_second(i):
+    def end_second(first, count):
+        here = pl.ds(first, count)
         for c in range(3):
-            total = adjd[c, i] + turn2[c, i]
-            turn2[c, i] = total
-            back = (0.25 * adjv[c, i] + 0.125 * total) * rden[i]
-            chan(BACK, c, 0)[i + 2, 8:24, :] = back
-        pack_plane(BACK, i, False)
-
-    inner_planes(end_second)
+            total = adjd[c, here] + turn2[c, here]
+            turn2[c, here] = total
+            back = (0.25 * adjv[c, here] + 0.125 * total) * rden[here]
+            chan(BACK, c, 0)[pl.ds(2 + first, count), 8:24, :] = back
+        pack_planes(BACK, first, count, False)
+
+    end_second(2, 4)
     for n in MESSAGES:
         sent[n].wait_send()
     for side in (0, 1):
@@ -574,21 +578,19 @@
             sent[n].wait_recv()
         take_radial(MOVED, side, False)
         cross_second(side)
-    outer_planes(end_second)
+    end_second(0, 2)
+    end_second(6, 2)
     pack_faces(BACK, False)
+    pack_corners(BACK)
 
     sent = copies(2)
     for n in MESSAGES:
         sent[n].start()
 
-    def velocities(i, carry):
-        for c in range(3):
-            accel = (force1[c, i] + force2[c, i]) * rden[i]
-            o_newv[c, i] = vel[c, i] + 0.25 * accel
-            o_gvel[c, i] = adjv[c, i] + 0.5 * turn2[c, i]
-        return carry
-
-    lax.fori_loop(0, NPL, velocities, 0)
+    for c in range(3):
+        accel = (force1[c] + force2[c]) * rden[...]
+        o_newv[c] = vel[c] + 0.25 * accel
+        o_gvel[c] = adjv[c] + 0.5 * turn2[c]
     outs = [
         pltpu.make_async_copy(o_newv, newv_h, store_sem.at[3]),
         pltpu.make_async_copy(o_gvel, gvel_h, store_sem.at[4]),
@@ -617,13 +619,9 @@
         take_radial(BACK, side, False)
         cross_third(side)
 
-    def finish(i, carry):
-        for c in range(3):
-            o_gdisp[c, i] = turn2[c, i] + turn3[c, i]
-        o_gmod[i] = -sens[i] / (mod[i] * mod[i])
-        return carry
-
-    lax.fori_loop(0, NPL, finish, 0)
+    for c in range(3):
+        o_gdisp[c] = turn2[c] + turn3[c]
+    o_gmod[...] = -sens[...] / (mod[...] * mod[...])
     last = [
         pltpu.make_async_copy(o_gdisp, gdisp_h, store_sem.at[5]),
         pltpu.make_async_copy(o_gmod, gmod_h, store_sem.at[6]),
@@ -683,7 +681,7 @@
         pltpu.SemaphoreType.DMA((53,)),
         pltpu.SemaphoreType.DMA((53,)),
     ]
-    return pl.pallas_call(
+    made = pl.pallas_call(
         kernel,
         out_shape=(
             shape(field, F32),
@@ -696,7 +694,7 @@
         out_specs=[anywhere] * 5,
         scratch_shapes=scratch,
         compiler_params=pltpu.CompilerParams(
-            collective_id=0, has_side_effects=True, vmem_limit_bytes=48 * 1024 * 1024
+            collective_id=0, has_side_effects=True, vmem_limit_bytes=62 * 1024 * 1024
         ),
         name="rock_wall_step",
     )(
@@ -709,6 +707,22 @@
         adjoint_disp,
         adjoint_vel,
     )
+    return pl.pallas_call(
+        hand_over,
+        out_shape=tuple(shape(x.shape, F32) for x in made),
+        in_specs=[anywhere] * 5,
+        out_specs=[anywhere] * 5,
+        scratch_shapes=[pltpu.SemaphoreType.DMA((5,))],
+        name="hand_over",
+    )(*made)
+
+
+def hand_over(*refs):
+    copies = [pltpu.make_async_copy(refs[j], refs[5 + j], refs[10].at[j]) for j in range(5)]
+    for copy in copies:
+        copy.start()
+    for copy in copies:
+        copy.wait()
 
 
 def solution(mesh):

time: 69.3 us -> 82.3 us (1.19)
  Pallas kernels: 57.3 us -> 81.5 us
  local copies, waits for them, and re-layouts: 11 us -> 0 us
    pallas_call x0 -> x1, Pallas kernels: none -> 27 us  [shards(): pl.pallas_call(hand_over, out_shape=tuple((shape(x.shape, F32) for x in m...]
    unnamed x21 -> x0, local copies, waits for them, and re-layouts: 11 us -> none
    pallas_call x1, Pallas kernels: 57.3 us -> 54.5 us  [shards(): pl.pallas_call(kernel, out_shape=(shape(field, F32), shape(field, F32), s...]
where the time goes in v2:
time: 82.3 us; the launch traced here: 82.1 us
  Pallas kernels  81.5 us (99%)
    pallas_call x1, Pallas kernels, shards(): pl.pallas_call(kernel, out_shape=(shape(field, F32), shape(field, F32), s...  54.5 us
    pallas_call x1, Pallas kernels, shards(): pl.pallas_call(hand_over, out_shape=tuple((shape(x.shape, F32) for x in m...  27 us

profile of v2, /device:TPU:1, one launch (start us, length us, event | category | flops | bytes accessed | tf_op | source)
XLA Modules:
  0.0 82.1 jit_solution(2477337920528265679)
XLA Ops:
  0.6 54.5 %rock_wall_step.1 = (f32[3,8,16,128]{3,2,1,0:T(8,128)}, f32[3,8,16,128]{3,2,1,0:T(8,128)}, f32[3,8,16,128]{3,2,1,0:T(8,128)}, f32[3,8,16,128]{3,2,1,0:T(8,128)}, f32[8,16,128]{2,1,0:T(8,128)}) custom-call(f32[3,8,16,128]{3,2,1,0:T(8,128)} %disp_h.1, f32[3,8,16,128]{3,2,1,0:T(8,128)} %vel_h.1, f32[8,16,128]{2,1,0:T(8,128)} %mod_h.1, s32[8,16,128]{2,1,0:T(8,128)} %cls_h.1, ...), custom_call_target="tpu_custom_call" | custom-call | tf_op jit(solution)/shard_map/rock_wall_step/pallas_call | solution.py:684
  55.2 27.0 %hand_over.1 = (f32[3,8,16,128]{3,2,1,0:T(8,128)}, f32[3,8,16,128]{3,2,1,0:T(8,128)}, f32[3,8,16,128]{3,2,1,0:T(8,128)}, f32[3,8,16,128]{3,2,1,0:T(8,128)}, f32[8,16,128]{2,1,0:T(8,128)}) custom-call(f32[3,8,16,128]{3,2,1,0:T(8,128)} %get-tuple-element.10.refs_0_, f32[3,8,16,128]{3,2,1,0:T(8,128)} %get-tuple-element.11.refs_1_, ...), custom_call_target="tpu_custom_call" | custom-call | tf_op jit(solution)/shard_map/hand_over/pallas_call | solution.py:710

commit v3 on v2

--- a/solution.py
+++ b/solution.py
@@ -26,8 +26,11 @@
     for da in (-1, 0, 1)
     if (da, dr, dd) != (0, 0, 0)
 ]
-MESSAGES = sorted(NEIGHBOURS, key=lambda n: (not (n[0] == 0 and n[2] == 0), abs(n[1])))
-NEAR = [n for n in MESSAGES if n[1] == 0]
+MESSAGES = sorted(NEIGHBOURS, key=lambda n: (abs(n[1]), n[2] if n[1] else 0, abs(n[0])))
+PARTNER = (0, 0, 1)
+NEAR = [n for n in MESSAGES if n[1] == 0 and n != PARTNER]
+ALONG = [k for k, o in enumerate(BOND_OFFSETS) if o[2] == 0]
+ACROSS = [k for k, o in enumerate(BOND_OFFSETS) if o[2] != 0]
 RADIAL = {
     side: [n for n in MESSAGES if n[1] == (-1 if side else 1)] for side in (0, 1)
 }
@@ -190,6 +193,8 @@
         parts = [near(t, c, offset, i) if offset[c] else None for c in range(3)]
         return signed(offset, parts) - signed(offset, cen)
 
+    own = pl.ds(2, NPL)
+
     def pack_planes(t, first, count, with_mod):
         at = pl.ds(2 + first, count)
         here = pl.ds(first, count)
@@ -298,35 +303,45 @@
     def turn_left(value, by):
         return pltpu.roll(value, lax.rem(2 * NLANE - by, NLANE), 1)
 
-    def take_own(t, with_mod):
+    def turned_arrays(t, with_mod):
+        for c in range(4 if with_mod else 3):
+            for r in (-2, -1, 1, 2) if c >= 2 else (-1, 1):
+                if c == 3:
+                    yield c, r, m.at[2 + r]
+                elif abs(r) == 2:
+                    yield c, r, w.at[SETS * 9 + t * 2 + (r > 0)]
+                else:
+                    yield c, r, chan(t, c, r)
+
+    def take_partner(t, with_mod):
+        tile = rd[t]
+        for c in range(4 if with_mod else 3):
+            to = m.at[2] if c == 3 else chan(t, c, 0)
+            to[own, pl.ds(halo_row, 1), :] = tile[:, c : c + 1]
+        chan(t, 1, 0)[own, pl.ds(halo_row2, 1), :] = tile[:, 4:5]
+        if with_mod:
+            m[2, own, pl.ds(halo_row2, 1), :] = tile[:, 5:6]
+        for c, r, to in turned_arrays(t, with_mod):
+            ref = m.at[2] if c == 3 else chan(t, c, 0)
+            to[own, 8:24, :] = pltpu.roll(ref[own, 8:24, :], (NLANE - r) % NLANE, 2)
+
+    def take_sides(t, with_mod):
         sides = both(rp[0, t], rp[1, t], lane)
         sides = jnp.stack(
             [pltpu.roll(sides, NLANE - 16 * i, 1) if i else sides for i in range(NPL)]
         )
         rows = spread(both(rpr[0, t], rpr[1, t], lane8[0:1]), 4, (1, 2))
         rows = jnp.stack([pltpu.roll(rows, NLANE - 16 * i - 2, 1) for i in range(NPL)])
+        for c, r, to in turned_arrays(t, with_mod):
+            edge = pltpu.roll(sides, (2 * NLANE - (4 * c + 2) - r) % NLANE, 2)
+            lanes = lane_all >= NLANE - r if r > 0 else lane_all < -r
+            to[own, 8:24, :] = jnp.where(lanes, edge, to[own, 8:24, :])
         tile = rd[t]
-        own = pl.ds(2, NPL)
-        for c in range(4 if with_mod else 3):
-            ref = m.at[2] if c == 3 else chan(t, c, 0)
-            value = ref[own, 8:24, :]
-            edge = pltpu.roll(sides, NLANE - (4 * c + 2), 2)
-            for r in (-2, -1, 1, 2) if c >= 2 else (-1, 1):
-                if c == 3:
-                    to = m.at[2 + r]
-                elif abs(r) == 2:
-                    to = w.at[SETS * 9 + t * 2 + (r > 0)]
-                else:
-                    to = chan(t, c, r)
-                to[own, 8:24, :] = shifted(value, edge, lane_all, r)
-        for r in (-1, 0, 1):
-            moved = tile if r == 0 else shifted(tile, rows, lane8_all, r)
+        for r in (-1, 1):
+            moved = shifted(tile, rows, lane8_all, r)
             for c in range(4 if with_mod else 3):
                 to = m.at[2 + r] if c == 3 else chan(t, c, r)
                 to[own, pl.ds(halo_row, 1), :] = moved[:, c : c + 1]
-        chan(t, 1, 0)[own, pl.ds(halo_row2, 1), :] = tile[:, 4:5]
-        if with_mod:
-            m[2, own, pl.ds(halo_row2, 1), :] = tile[:, 5:6]
 
     def take_radial(t, side, with_mod):
         at, far = (10, 11) if side else (1, 0)
@@ -457,20 +472,13 @@
                     turn3[c, i] = turns[c]
             sens[i] = total
 
-    own = pl.ds(2, NPL)
     sent = copies(0)
     sent_carried = carried_copies()
-    loads["disp"].wait()
-    loads["mod"].wait()
+    for name in ("disp", "mod", "cls", "adjv"):
+        loads[name].wait()
     m[2, own, 8:24, :] = mod[...]
     for c in range(3):
         chan(DISP, c, 0)[own, 8:24, :] = disp[c]
-    pack_faces(DISP, True)
-    pl.semaphore_wait(barrier, len(NEIGHBOURS))
-    for n in MESSAGES[:2]:
-        sent[n].start()
-    loads["cls"].wait()
-    loads["adjv"].wait()
     kinds = cls[...]
     density = jnp.full((NPL, NROW, NLANE), dens[0])
     for level in range(1, 8):
@@ -478,33 +486,39 @@
     rden[...] = 1.0 / density
     for c in range(3):
         chan(CARRIED, c, 0)[own, 8:24, :] = 0.25 * adjv[c] * rden[...]
-    pack_planes(DISP, 0, NPL, True)
-    pack_planes(CARRIED, 0, NPL, False)
-    pack_corners(DISP)
-    pack_corners(CARRIED)
-    pack_faces(CARRIED, False)
-    for n in MESSAGES[2:]:
+    for t in (DISP, CARRIED):
+        pack_planes(t, 0, NPL, t == DISP)
+        pack_faces(t, t == DISP)
+        pack_corners(t)
+    pl.semaphore_wait(barrier, len(NEIGHBOURS))
+    for n in MESSAGES:
         sent[n].start()
     for side in (0, 1):
         sent_carried[side].start()
     for name in ("bi", "vel", "adjd"):
         loads[name].wait()
+
+    def sweep_first(bonds, fresh):
+        def plane(i, carry):
+            cen, cm = centre(DISP, i), m[2, i + 2, 8:24, :]
+            forces = zeros(3) if fresh else [force1[c, i] for c in range(3)]
+            for k in bonds:
+                forces, made = bond_first(BOND_OFFSETS[k], i, cen, cm, bi[k, i], forces)
+                for ref, value in zip((ecoef, gcoef, acoef, bcoef), made):
+                    ref[k, i] = value
+            for c in range(3):
+                force1[c, i] = forces[c]
+            return carry
+
+        lax.fori_loop(0, NPL, plane, 0)
+
+    sent[PARTNER].wait_recv()
+    take_partner(DISP, True)
+    sweep_first(ALONG, True)
     for n in NEAR:
         sent[n].wait_recv()
-    take_own(DISP, True)
-    take_own(CARRIED, False)
-
-    def sweep_first(i, carry):
-        cen, cm, forces = centre(DISP, i), m[2, i + 2, 8:24, :], zeros(3)
-        for k, offset in enumerate(BOND_OFFSETS):
-            forces, made = bond_first(offset, i, cen, cm, bi[k, i], forces)
-            for ref, value in zip((ecoef, gcoef, acoef, bcoef), made):
-                ref[k, i] = value
-        for c in range(3):
-            force1[c, i] = forces[c]
-        return carry
-
-    lax.fori_loop(0, NPL, sweep_first, 0)
+    take_sides(DISP, True)
+    sweep_first(ACROSS, False)
 
     def end_first(first, count):
         here = pl.ds(first, count)
@@ -538,28 +552,41 @@
     ]
     for copy in moved_out:
         copy.start()
+    sent[PARTNER].wait_recv()
+    take_partner(MOVED, False)
+    take_partner(CARRIED, False)
+    take_sides(CARRIED, False)
     for side in (0, 1):
         sent_carried[side].wait_recv()
         sent_carried[side].wait_send()
         take_radial(CARRIED, side, False)
+
+    def sweep_second(bonds, fresh):
+        def plane(i, carry):
+            cen, cen_z = centre(MOVED, i), centre(CARRIED, i)
+            if fresh:
+                forces, turns, total = zeros(3), zeros(3), zeros(1)[0]
+            else:
+                forces = [force2[c, i] for c in range(3)]
+                turns = [turn2[c, i] for c in range(3)]
+                total = sens[i]
+            for k in bonds:
+                forces, turns, total = bond_second(
+                    BOND_OFFSETS[k], i, cen, cen_z, ecoef[k, i], gcoef[k, i], forces, turns, total
+                )
+            for c in range(3):
+                force2[c, i] = forces[c]
+                turn2[c, i] = turns[c]
+            sens[i] = total
+            return carry
+
+        lax.fori_loop(0, NPL, plane, 0)
+
+    sweep_second(ALONG, True)
     for n in NEAR:
         sent[n].wait_recv()
-    take_own(MOVED, False)
-
-    def sweep_second(i, carry):
-        cen, cen_z = centre(MOVED, i), centre(CARRIED, i)
-        forces, turns, total = zeros(3), zeros(3), zeros(1)[0]
-        for k, offset in enumerate(BOND_OFFSETS):
-            forces, turns, total = bond_second(
-                offset, i, cen, cen_z, ecoef[k, i], gcoef[k, i], forces, turns, total
-            )
-        for c in range(3):
-            force2[c, i] = forces[c]
-            turn2[c, i] = turns[c]
-        sens[i] = total
-        return carry
-
-    lax.fori_loop(0, NPL, sweep_second, 0)
+    take_sides(MOVED, False)
+    sweep_second(ACROSS, False)
 
     def end_second(first, count):
         here = pl.ds(first, count)
@@ -597,20 +624,28 @@
     ]
     for copy in outs:
         copy.start()
+    def sweep_third(bonds, fresh):
+        def plane(i, carry):
+            cen_z, total = centre(BACK, i), sens[i]
+            turns = zeros(3) if fresh else [turn3[c, i] for c in range(3)]
+            for k in bonds:
+                turns, total = bond_third(
+                    BOND_OFFSETS[k], i, cen_z, acoef[k, i], bcoef[k, i], turns, total
+                )
+            for c in range(3):
+                turn3[c, i] = turns[c]
+            sens[i] = total
+            return carry
+
+        lax.fori_loop(0, NPL, plane, 0)
+
+    sent[PARTNER].wait_recv()
+    take_partner(BACK, False)
+    sweep_third(ALONG, True)
     for n in NEAR:
         sent[n].wait_recv()
-    take_own(BACK, False)
-
-    def sweep_third(i, carry):
-        cen_z, turns, total = centre(BACK, i), zeros(3), sens[i]
-        for k, offset in enumerate(BOND_OFFSETS):
-            turns, total = bond_third(offset, i, cen_z, acoef[k, i], bcoef[k, i], turns, total)
-        for c in range(3):
-            turn3[c, i] = turns[c]
-        sens[i] = total
-        return carry
-
-    lax.fori_loop(0, NPL, sweep_third, 0)
+    take_sides(BACK, False)
+    sweep_third(ACROSS, False)
     for n in MESSAGES:
         sent[n].wait_send()
     for side in (0, 1):
@@ -712,16 +747,21 @@
         out_shape=tuple(shape(x.shape, F32) for x in made),
         in_specs=[anywhere] * 5,
         out_specs=[anywhere] * 5,
-        scratch_shapes=[pltpu.SemaphoreType.DMA((5,))],
+        scratch_shapes=[vmem(x.shape, F32) for x in made] + [pltpu.SemaphoreType.DMA((2, 5))],
         name="hand_over",
     )(*made)
 
 
 def hand_over(*refs):
-    copies = [pltpu.make_async_copy(refs[j], refs[5 + j], refs[10].at[j]) for j in range(5)]
-    for copy in copies:
+    given, outs, held, sems = refs[:5], refs[5:10], refs[10:15], refs[15]
+    inward = [pltpu.make_async_copy(given[j], held[j], sems.at[0, j]) for j in range(5)]
+    outward = [pltpu.make_async_copy(held[j], outs[j], sems.at[1, j]) for j in range(5)]
+    for copy in inward:
         copy.start()
-    for copy in copies:
+    for j in range(5):
+        inward[j].wait()
+        outward[j].start()
+    for copy in outward:
         copy.wait()
 
 

time: 82.3 us -> 55.7 us (0.68)
  Pallas kernels: 81.5 us -> 54.9 us
    pallas_call x1, Pallas kernels: 27 us -> 2 us  [shards(): pl.pallas_call(hand_over, out_shape=tuple((shape(x.shape, F32) for x in m...]
    pallas_call x1, Pallas kernels: 54.5 us -> 52.9 us  [shards(): pl.pallas_call(kernel, out_shape=(shape(field, F32), shape(field, F32), s...]
where the time goes in v3:
time: 55.7 us; the launch traced here: 55.5 us
  Pallas kernels  54.9 us (99%)
  between operations  0.64 us (1%)
    pallas_call x1, Pallas kernels, shards(): pl.pallas_call(kernel, out_shape=(shape(field, F32), shape(field, F32), s...  52.9 us
    pallas_call x1, Pallas kernels, shards(): pl.pallas_call(hand_over, out_shape=tuple((shape(x.shape, F32) for x in m...  2 us

profile of v3, /device:TPU:1, one launch (start us, length us, event | category | flops | bytes accessed | tf_op | source)
XLA Modules:
  0.0 55.5 jit_solution(14806092679931172997)
XLA Ops:
  0.6 52.9 %rock_wall_step.1 = (f32[3,8,16,128]{3,2,1,0:T(8,128)}, f32[3,8,16,128]{3,2,1,0:T(8,128)}, f32[3,8,16,128]{3,2,1,0:T(8,128)}, f32[3,8,16,128]{3,2,1,0:T(8,128)}, f32[8,16,128]{2,1,0:T(8,128)}) custom-call(f32[3,8,16,128]{3,2,1,0:T(8,128)} %disp_h.1, f32[3,8,16,128]{3,2,1,0:T(8,128)} %vel_h.1, f32[8,16,128]{2,1,0:T(8,128)} %mod_h.1, s32[8,16,128]{2,1,0:T(8,128)} %cls_h.1, ...), custom_call_target="tpu_custom_call" | custom-call | tf_op jit(solution)/shard_map/rock_wall_step/pallas_call | solution.py:719
  53.5 2.0 %hand_over.1 = (f32[3,8,16,128]{3,2,1,0:T(8,128)}, f32[3,8,16,128]{3,2,1,0:T(8,128)}, f32[3,8,16,128]{3,2,1,0:T(8,128)}, f32[3,8,16,128]{3,2,1,0:T(8,128)}, f32[8,16,128]{2,1,0:T(8,128)}) custom-call(f32[3,8,16,128]{3,2,1,0:T(8,128)} %get-tuple-element.10.refs_0_, f32[3,8,16,128]{3,2,1,0:T(8,128)} %get-tuple-element.11.refs_1_, ...), custom_call_target="tpu_custom_call" | custom-call | tf_op jit(solution)/shard_map/hand_over/pallas_call | solution.py:745

commit v4 on v3

--- a/solution.py
+++ b/solution.py
@@ -26,7 +26,11 @@
     for da in (-1, 0, 1)
     if (da, dr, dd) != (0, 0, 0)
 ]
-MESSAGES = sorted(NEIGHBOURS, key=lambda n: (abs(n[1]), n[2] if n[1] else 0, abs(n[0])))
+FACES = [(0, -1, 0), (0, 1, 0)]
+REST = sorted(
+    (n for n in NEIGHBOURS if n not in FACES), key=lambda n: (-abs(n[1]), n[2] if n[1] else 0, -abs(n[0]))
+)
+MESSAGES = FACES + REST
 PARTNER = (0, 0, 1)
 NEAR = [n for n in MESSAGES if n[1] == 0 and n != PARTNER]
 ALONG = [k for k, o in enumerate(BOND_OFFSETS) if o[2] == 0]
@@ -94,10 +98,6 @@
     turn2,
     turn3,
     sens,
-    o_newv,
-    o_gvel,
-    o_gdisp,
-    o_gmod,
     pack,
     sd,
     se,
@@ -110,7 +110,6 @@
     re,
     rer,
     load_sem,
-    store_sem,
     send_sem,
     recv_sem,
 ):
@@ -215,8 +214,8 @@
             packed = jnp.where(lane // 16 == i, rolled, packed)
         pack[t] = packed
 
-    def pack_faces(t, with_mod):
-        for side in (0, 1):
+    def pack_faces(t, with_mod, sides=(0, 1)):
+        for side in sides:
             outer, inner = (9, 8) if side else (2, 3)
             for c in range(3):
                 sf[side, t, c] = chan(t, c, 0)[outer, 8:24, :]
@@ -526,32 +525,29 @@
             accel = force1[c, here] * rden[here]
             moved = disp[c, here] + 0.5 * vel[c, here] + 0.125 * accel
             chan(MOVED, c, 0)[pl.ds(2 + first, count), 8:24, :] = moved
-        pack_planes(MOVED, first, count, False)
 
     end_first(2, 4)
+    pack_planes(MOVED, 2, 4, False)
     for n in MESSAGES:
         sent[n].wait_send()
+    following = copies(1)
     for side in (0, 1):
         for n in RADIAL[side]:
             sent[n].wait_recv()
         take_radial(DISP, side, True)
         cross_first(side)
-    end_first(0, 2)
-    end_first(6, 2)
-    pack_faces(MOVED, False)
+        end_first(6 * side, 2)
+        pack_faces(MOVED, False, (side,))
+        following[FACES[side]].start()
+    sent = following
+
+    pack_planes(MOVED, 0, 2, False)
+    pack_planes(MOVED, 6, 2, False)
     pack_corners(MOVED)
-
-    sent = copies(1)
-    for n in MESSAGES:
+    for n in REST:
         sent[n].start()
-    moved_out = [
-        pltpu.make_async_copy(
-            chan(MOVED, c, 0).at[pl.ds(2, NPL), pl.ds(8, NROW)], moved_h.at[c], store_sem.at[c]
-        )
-        for c in range(3)
-    ]
-    for copy in moved_out:
-        copy.start()
+    for c in range(3):
+        moved_h[c] = chan(MOVED, c, 0)[own, 8:24, :]
     sent[PARTNER].wait_recv()
     take_partner(MOVED, False)
     take_partner(CARRIED, False)
@@ -595,35 +591,32 @@
             turn2[c, here] = total
             back = (0.25 * adjv[c, here] + 0.125 * total) * rden[here]
             chan(BACK, c, 0)[pl.ds(2 + first, count), 8:24, :] = back
-        pack_planes(BACK, first, count, False)
 
     end_second(2, 4)
+    pack_planes(BACK, 2, 4, False)
     for n in MESSAGES:
         sent[n].wait_send()
+    following = copies(2)
     for side in (0, 1):
         for n in RADIAL[side]:
             sent[n].wait_recv()
         take_radial(MOVED, side, False)
         cross_second(side)
-    end_second(0, 2)
-    end_second(6, 2)
-    pack_faces(BACK, False)
+        end_second(6 * side, 2)
+        pack_faces(BACK, False, (side,))
+        following[FACES[side]].start()
+    sent = following
+
+    pack_planes(BACK, 0, 2, False)
+    pack_planes(BACK, 6, 2, False)
     pack_corners(BACK)
-
-    sent = copies(2)
-    for n in MESSAGES:
+    for n in REST:
         sent[n].start()
 
     for c in range(3):
         accel = (force1[c] + force2[c]) * rden[...]
-        o_newv[c] = vel[c] + 0.25 * accel
-        o_gvel[c] = adjv[c] + 0.5 * turn2[c]
-    outs = [
-        pltpu.make_async_copy(o_newv, newv_h, store_sem.at[3]),
-        pltpu.make_async_copy(o_gvel, gvel_h, store_sem.at[4]),
-    ]
-    for copy in outs:
-        copy.start()
+        newv_h[c] = vel[c] + 0.25 * accel
+        gvel_h[c] = adjv[c] + 0.5 * turn2[c]
     def sweep_third(bonds, fresh):
         def plane(i, carry):
             cen_z, total = centre(BACK, i), sens[i]
@@ -646,6 +639,14 @@
         sent[n].wait_recv()
     take_sides(BACK, False)
     sweep_third(ACROSS, False)
+
+    def finish(first, count):
+        here = pl.ds(first, count)
+        for c in range(3):
+            gdisp_h[c, here] = turn2[c, here] + turn3[c, here]
+        gmod_h[here] = -sens[here] / (mod[here] * mod[here])
+
+    finish(2, 4)
     for n in MESSAGES:
         sent[n].wait_send()
     for side in (0, 1):
@@ -653,18 +654,7 @@
             sent[n].wait_recv()
         take_radial(BACK, side, False)
         cross_third(side)
-
-    for c in range(3):
-        o_gdisp[c] = turn2[c] + turn3[c]
-    o_gmod[...] = -sens[...] / (mod[...] * mod[...])
-    last = [
-        pltpu.make_async_copy(o_gdisp, gdisp_h, store_sem.at[5]),
-        pltpu.make_async_copy(o_gmod, gmod_h, store_sem.at[6]),
-    ]
-    for copy in last:
-        copy.start()
-    for copy in moved_out + outs + last:
-        copy.wait()
+        finish(6 * side, 2)
 
 
 def shards(
@@ -696,10 +686,6 @@
         vmem(field, F32),
         vmem(field, F32),
         vmem(block, F32),
-        vmem(field, F32),
-        vmem(field, F32),
-        vmem(field, F32),
-        vmem(block, F32),
         vmem((SETS, NROW, NLANE), F32),
         vmem((SETS, NPL, 8, NLANE), F32),
         vmem((2, SETS, 2, NLANE), F32),
@@ -712,24 +698,23 @@
         vmem((2, 2, SETS, 2, NLANE), F32),
         vmem((2, 2, SETS, 1, NLANE), F32),
         pltpu.SemaphoreType.DMA((7,)),
-        pltpu.SemaphoreType.DMA((7,)),
         pltpu.SemaphoreType.DMA((53,)),
         pltpu.SemaphoreType.DMA((53,)),
     ]
     made = pl.pallas_call(
         kernel,
         out_shape=(
-            shape(field, F32),
-            shape(field, F32),
-            shape(field, F32),
-            shape(field, F32),
-            shape(block, F32),
+            vmem(field, F32),
+            vmem(field, F32),
+            vmem(field, F32),
+            vmem(field, F32),
+            vmem(block, F32),
         ),
         in_specs=[anywhere] * 5 + [pl.BlockSpec(memory_space=pltpu.SMEM)] + [anywhere] * 2,
-        out_specs=[anywhere] * 5,
+        out_specs=[pl.BlockSpec(memory_space=vmem)] * 5,
         scratch_shapes=scratch,
         compiler_params=pltpu.CompilerParams(
-            collective_id=0, has_side_effects=True, vmem_limit_bytes=62 * 1024 * 1024
+            collective_id=0, has_side_effects=True, vmem_limit_bytes=54 * 1024 * 1024
         ),
         name="rock_wall_step",
     )(
@@ -745,23 +730,18 @@
     return pl.pallas_call(
         hand_over,
         out_shape=tuple(shape(x.shape, F32) for x in made),
-        in_specs=[anywhere] * 5,
+        in_specs=[pl.BlockSpec(memory_space=vmem)] * 5,
         out_specs=[anywhere] * 5,
-        scratch_shapes=[vmem(x.shape, F32) for x in made] + [pltpu.SemaphoreType.DMA((2, 5))],
+        scratch_shapes=[pltpu.SemaphoreType.DMA((5,))],
         name="hand_over",
-    )(*made)
+    )(*[pltpu.with_memory_space_constraint(x, vmem) for x in made])
 
 
 def hand_over(*refs):
-    given, outs, held, sems = refs[:5], refs[5:10], refs[10:15], refs[15]
-    inward = [pltpu.make_async_copy(given[j], held[j], sems.at[0, j]) for j in range(5)]
-    outward = [pltpu.make_async_copy(held[j], outs[j], sems.at[1, j]) for j in range(5)]
-    for copy in inward:
+    copies = [pltpu.make_async_copy(refs[j], refs[5 + j], refs[10].at[j]) for j in range(5)]
+    for copy in copies:
         copy.start()
-    for j in range(5):
-        inward[j].wait()
-        outward[j].start()
-    for copy in outward:
+    for copy in copies:
         copy.wait()
 
 

time: 55.7 us -> 52.7 us (0.946)
  Pallas kernels: 54.9 us -> 51.9 us
    pallas_call x1, Pallas kernels: 52.9 us -> 51 us  [shards(): pl.pallas_call(kernel, out_shape=(vmem(field, F32), vmem(field, F32), vme...]
    pallas_call x1, Pallas kernels: 2 us -> 0.93 us  [shards(): pl.pallas_call(hand_over, out_shape=tuple((shape(x.shape, F32) for x in m...]
where the time goes in v4:
time: 52.7 us; the launch traced here: 52.6 us
  Pallas kernels  51.9 us (98%)
  between operations  0.64 us (1%)
    pallas_call x1, Pallas kernels, shards(): pl.pallas_call(kernel, out_shape=(vmem(field, F32), vmem(field, F32), vme...  51 us

profile of v4, /device:TPU:1, one launch (start us, length us, event | category | flops | bytes accessed | tf_op | source)
XLA Modules:
  0.0 52.6 jit_solution(18215488700278405092)
XLA Ops:
  0.6 51.0 %rock_wall_step.1 = (f32[3,8,16,128]{3,2,1,0:T(8,128)S(1)}, f32[3,8,16,128]{3,2,1,0:T(8,128)S(1)}, f32[3,8,16,128]{3,2,1,0:T(8,128)S(1)}, f32[3,8,16,128]{3,2,1,0:T(8,128)S(1)}, f32[8,16,128]{2,1,0:T(8,128)S(1)}) custom-call(f32[3,8,16,128]{3,2,1,0:T(8,128)} %disp_h.1, f32[3,8,16,128]{3,2,1,0:T(8,128)} %vel_h.1, f32[8,16,128]{2,1,0:T(8,128)} %mod_h.1, ...), custom_call_target="tpu_custom_call" | custom-call | tf_op jit(solution)/shard_map/rock_wall_step/pallas_call | solution.py:704
  51.6 0.9 %hand_over.1 = (f32[3,8,16,128]{3,2,1,0:T(8,128)}, f32[3,8,16,128]{3,2,1,0:T(8,128)}, f32[3,8,16,128]{3,2,1,0:T(8,128)}, f32[3,8,16,128]{3,2,1,0:T(8,128)}, f32[8,16,128]{2,1,0:T(8,128)}) custom-call(f32[3,8,16,128]{3,2,1,0:T(8,128)S(1)} %get-tuple-element.10.refs_0_, f32[3,8,16,128]{3,2,1,0:T(8,128)S(1)} %get-tuple-element.11.refs_1_, ...), custom_call_target="tpu_custom_call" | custom-call | tf_op jit(solution)/shard_map/hand_over/pallas_call | solution.py:730
